TPU v7x, 32 devices: a whole 2x2x4 slice. The times are simulated.
32 devices in a mesh: dp: 8 (over z, x), tensor: 4 (over y, core).
Axes of the slice: x: 2, y: 2, z: 4, core: 2. Of those that a mesh axis runs over, the one named last changes fastest.
Arguments:
- block_input: float32 [18912, 768], P(('dp', 'tensor')), may hold values from -6 to 6
- cotangent: float32 [18912, 768], P(('dp', 'tensor')), may hold values from -6 to 6
- query_weight: float32 [768, 768], P('dp', 'tensor'), may hold values from -0.21875 to 0.21875
- key_weight: float32 [768, 768], P('dp', 'tensor'), may hold values from -0.21875 to 0.21875
- value_weight: float32 [768, 768], P('dp', 'tensor'), may hold values from -0.21875 to 0.21875
- output_weight: float32 [768, 768], P('tensor', 'dp'), may hold values from -1.75 to 1.75
- first_gain: float32 [768], P('dp'), may hold values from 0.5 to 1.5
- first_shift: float32 [768], P('dp'), may hold values from -1 to 1
- expert_in: float32 [8, 768, 3072], P(None, 'dp', 'tensor'), may hold values from -0.21875 to 0.21875
- expert_out: float32 [8, 3072, 768], P(None, 'tensor', 'dp'), may hold values from -0.21875 to 0.21875
- second_gain: float32 [768], P('dp'), may hold values from 0.5 to 1.5
- second_shift: float32 [768], P('dp'), may hold values from -1 to 1
- routes: int32 [18912, 2], P('dp'), may hold values from 0 to 7, all different within a row; in each aligned block of 2364 rows (0 to 2363, 2364 to 4727, ...) at most 792 rows name the same one
- route_gates: float32 [18912, 2], P('dp'), may hold values from 0.25 to 0.75
- clip_threshold: float32 [12], P('tensor'), may hold values from 3 to 9
Outputs:
- block_output: float32 [18912, 768], P(('dp', 'tensor'))
- input_grad: float32 [18912, 768], P(('dp', 'tensor'))
- query_grad: float32 [768, 768], P('dp', 'tensor')
- key_grad: float32 [768, 768], P('dp', 'tensor')
- value_grad: float32 [768, 768], P('dp', 'tensor')
- output_grad: float32 [768, 768], P('tensor', 'dp')
- first_gain_grad: float32 [768], P('dp')
- first_shift_grad: float32 [768], P('dp')
- expert_in_grad: float32 [8, 768, 3072], P(None, 'dp', 'tensor')
- expert_out_grad: float32 [8, 3072, 768], P(None, 'tensor', 'dp')
- second_gain_grad: float32 [768], P('dp')
- second_shift_grad: float32 [768], P('dp')
- clipped_query: float32 [768, 768], P('dp', 'tensor')
- clipped_key: float32 [768, 768], P('dp', 'tensor')
- head_maxima: float32 [12], P('tensor')
Inputs may be any that keep to these rules, and one draw needn't show every extreme that they name: `routes`: each row names two different experts. In each aligned block of 2364 rows (the tokens of one index of dp) no expert is named by more than 792 rows, a bound that some block reaches.
All inputs are finite; a program needn't handle non-finite values.
Results may differ from a plain program's by a relative error of at most 0.018.
Values may be sent and summed in bfloat16 or wider, within the bound.
No kernel may reach another device: no remote copies, remote signals or barrier semaphores. Data moves between devices by JAX's collectives and lax.ppermute only.
A program may use at most 320 MiB of HBM per device.

v0:
```python
import math

import jax
import jax.numpy as jnp
from jax import lax
from jax.sharding import PartitionSpec as P

HD = 64
SEQ = 197
CAP = 792


EPSILON = 1e-06


def layer_norm(values, gain_row, shift_row):
    row_mean = jnp.mean(values, -1, keepdims=True)
    centred = values - row_mean
    spread = jnp.mean(centred * centred, -1, keepdims=True)
    return centred * lax.rsqrt(spread + EPSILON) * gain_row + shift_row


def gelu_exact(values):
    return jax.nn.gelu(values, approximate=False)


def to_half(values):
    return values.astype(jnp.bfloat16)


def expert_params(expert_in, expert_out, second_gain, second_shift):
    return (
        lax.all_gather(to_half(expert_in), "dp", axis=1, tiled=True),
        lax.all_gather(to_half(expert_out), "dp", axis=2, tiled=True),
        lax.all_gather(to_half(second_gain), "dp", axis=0, tiled=True),
        lax.all_gather(to_half(second_shift), "dp", axis=0, tiled=True),
    )


def score_block(query_heads, key_heads, score_scale):
    return (
        jnp.einsum("ishd,ithd->ihst", query_heads, key_heads, preferred_element_type=jnp.float32)
        * score_scale
    )


def slot_tables(route_ids, route_weights, capacity, experts):
    picks = route_ids.shape[1]
    flat_ids = route_ids.reshape(-1)
    onehot = (flat_ids[:, None] == jnp.arange(experts, dtype=jnp.int32)[None, :]).astype(jnp.int32)
    before = jnp.cumsum(onehot, 0) - onehot
    position = jnp.sum(before * onehot, 1)
    slot_of_route = flat_ids * capacity + position
    route_token = jnp.arange(flat_ids.shape[0], dtype=jnp.int32) // picks
    slot_token = jnp.zeros((experts * capacity,), jnp.int32).at[slot_of_route].set(route_token)
    slot_gate = (
        jnp.zeros((experts * capacity,), jnp.float32)
        .at[slot_of_route]
        .set(route_weights.reshape(-1))
    )
    return (slot_of_route, slot_token, slot_gate)


def expert_math(slot_rows, slot_cot, weight_in, weight_out):
    hidden_pre = jnp.einsum(
        "ecd,edf->ecf", slot_rows, weight_in, preferred_element_type=jnp.float32
    )
    activated = to_half(gelu_exact(hidden_pre))
    produced = jnp.einsum("ecf,efd->ecd", activated, weight_out, preferred_element_type=jnp.float32)
    grad_down = jnp.einsum("ecf,ecd->efd", activated, slot_cot, preferred_element_type=jnp.float32)
    grad_act = jnp.einsum("ecd,efd->ecf", slot_cot, weight_out, preferred_element_type=jnp.float32)
    _, slope_back = jax.vjp(gelu_exact, hidden_pre)
    grad_pre_half = to_half(slope_back(grad_act)[0])
    grad_up = jnp.einsum(
        "ecd,ecf->edf", slot_rows, grad_pre_half, preferred_element_type=jnp.float32
    )
    grad_slots = jnp.einsum(
        "ecf,edf->ecd", grad_pre_half, weight_in, preferred_element_type=jnp.float32
    )
    return (produced, grad_slots, grad_up, grad_down)


def body(
    block_input,
    cotangent,
    query_weight,
    key_weight,
    value_weight,
    output_weight,
    first_gain,
    first_shift,
    expert_in,
    expert_out,
    second_gain,
    second_shift,
    routes,
    route_gates,
    clip_threshold,
):
    features = block_input.shape[1]
    columns = query_weight.shape[1]
    heads_here = columns // HD
    group_rows = routes.shape[0]
    picks = routes.shape[1]
    images = group_rows // SEQ
    experts = expert_in.shape[0]
    score_scale = 1.0 / math.sqrt(HD)
    query_full, key_full, value_full, output_full, gain_one, shift_one = (
        lax.all_gather(to_half(query_weight), "dp", axis=0, tiled=True),
        lax.all_gather(to_half(key_weight), "dp", axis=0, tiled=True),
        lax.all_gather(to_half(value_weight), "dp", axis=0, tiled=True),
        lax.all_gather(to_half(output_weight), "dp", axis=1, tiled=True),
        lax.all_gather(to_half(first_gain), "dp", axis=0, tiled=True),
        lax.all_gather(to_half(first_shift), "dp", axis=0, tiled=True),
    )
    gain_one_f = gain_one.astype(jnp.float32)
    shift_one_f = shift_one.astype(jnp.float32)
    normed = layer_norm(block_input, gain_one_f, shift_one_f)
    gathered = lax.all_gather(to_half(normed), "tensor", axis=0, tiled=True)
    project_in = jnp.concatenate((query_full, key_full, value_full), 1)
    qkv_half = to_half(jnp.dot(gathered, project_in, preferred_element_type=jnp.float32))
    query_heads = qkv_half[:, :columns].reshape(images, SEQ, heads_here, HD)
    key_heads = qkv_half[:, columns : 2 * columns].reshape(images, SEQ, heads_here, HD)
    value_heads = qkv_half[:, 2 * columns :].reshape(images, SEQ, heads_here, HD)
    scores = score_block(query_heads, key_heads, score_scale)
    local_max = jnp.max(scores, axis=(0, 2, 3))
    row_top = jnp.max(scores, -1, keepdims=True)
    exponent = jnp.exp(scores - row_top)
    row_total = jnp.sum(exponent, -1, keepdims=True)
    log_total = row_top + jnp.log(row_total)
    attention = exponent / row_total
    mixed_heads = jnp.einsum(
        "ihst,ithd->ishd", to_half(attention), value_heads, preferred_element_type=jnp.float32
    )
    mixed_half = to_half(mixed_heads.reshape(group_rows, columns))
    partial_value = jnp.dot(mixed_half, output_full, preferred_element_type=jnp.float32)
    attended = lax.psum_scatter(
        partial_value.astype(jnp.bfloat16), "tensor", scatter_dimension=0, tiled=True
    ).astype(jnp.float32)
    residual = block_input + attended
    head_maxima = lax.pmax(local_max, "dp")
    expert_in_full, expert_out_full, gain_two, shift_two = expert_params(
        expert_in, expert_out, second_gain, second_shift
    )
    gain_two_f = gain_two.astype(jnp.float32)
    shift_two_f = shift_two.astype(jnp.float32)
    normed_two = layer_norm(residual, gain_two_f, shift_two_f)
    gathered_two = lax.all_gather(to_half(normed_two), "tensor", axis=0, tiled=True)
    cotangent_rows = lax.all_gather(to_half(cotangent), "tensor", axis=0, tiled=True)
    slot_of_route, slot_token, slot_gate = slot_tables(routes, route_gates, CAP, experts)
    slot_rows = jnp.take(gathered_two, slot_token, axis=0).reshape(experts, CAP, features)
    slot_cot = to_half(
        jnp.take(cotangent_rows, slot_token, axis=0).astype(jnp.float32) * slot_gate[:, None]
    ).reshape(experts, CAP, features)
    produced, grad_slots, grad_up, grad_down = expert_math(
        slot_rows, slot_cot, expert_in_full, expert_out_full
    )
    picked = jnp.take(produced.reshape(experts * CAP, features), slot_of_route, axis=0).reshape(
        group_rows, picks, features
    )
    combined = jnp.sum(picked * route_gates[:, :, None], 1)
    mixture = lax.psum_scatter(
        combined.astype(jnp.bfloat16), "tensor", scatter_dimension=0, tiled=True
    ).astype(jnp.float32)
    grad_normed_part = jnp.sum(
        jnp.take(grad_slots.reshape(experts * CAP, features), slot_of_route, axis=0).reshape(
            group_rows, picks, features
        ),
        1,
    )
    grad_normed_two = lax.psum_scatter(
        grad_normed_part.astype(jnp.bfloat16), "tensor", scatter_dimension=0, tiled=True
    ).astype(jnp.float32)
    block_output = residual + mixture
    _, norm_back_two = jax.vjp(layer_norm, residual, gain_two_f, shift_two_f)
    grad_resid_norm, grad_gain_two, grad_shift_two = norm_back_two(grad_normed_two)
    expert_in_grad, expert_out_grad, gain_two_share, shift_two_share = (
        lax.psum_scatter(grad_up, "dp", scatter_dimension=1, tiled=True),
        lax.psum_scatter(grad_down, "dp", scatter_dimension=2, tiled=True),
        lax.psum_scatter(grad_gain_two, "dp", scatter_dimension=0, tiled=True),
        lax.psum_scatter(grad_shift_two, "dp", scatter_dimension=0, tiled=True),
    )
    grad_resid = cotangent + grad_resid_norm
    grad_rows = lax.all_gather(to_half(grad_resid), "tensor", axis=0, tiled=True)
    grad_mixed = to_half(
        jnp.einsum("rd,cd->rc", grad_rows, output_full, preferred_element_type=jnp.float32)
    )
    grad_output_part = jnp.einsum(
        "rc,rd->cd", mixed_half, grad_rows, preferred_element_type=jnp.float32
    )
    grad_heads = grad_mixed.reshape(images, SEQ, heads_here, HD)
    attention_again = jnp.exp(score_block(query_heads, key_heads, score_scale) - log_total)
    grad_attention = jnp.einsum(
        "ishd,ithd->ihst", grad_heads, value_heads, preferred_element_type=jnp.float32
    )
    grad_values = jnp.einsum(
        "ihst,ishd->ithd", to_half(attention_again), grad_heads, preferred_element_type=jnp.float32
    )
    inner_sum = jnp.sum(attention_again * grad_attention, -1, keepdims=True)
    grad_scores = to_half(attention_again * (grad_attention - inner_sum))
    grad_queries = (
        jnp.einsum("ihst,ithd->ishd", grad_scores, key_heads, preferred_element_type=jnp.float32)
        * score_scale
    )
    grad_keys = (
        jnp.einsum("ihst,ishd->ithd", grad_scores, query_heads, preferred_element_type=jnp.float32)
        * score_scale
    )
    grad_qkv = to_half(
        jnp.concatenate(
            (
                grad_queries.reshape(group_rows, columns),
                grad_keys.reshape(group_rows, columns),
                grad_values.reshape(group_rows, columns),
            ),
            1,
        )
    )
    grad_project = jnp.einsum("rd,rc->dc", gathered, grad_qkv, preferred_element_type=jnp.float32)
    grad_normed_one_part = jnp.einsum(
        "rc,dc->rd", grad_qkv, project_in, preferred_element_type=jnp.float32
    )
    grad_normed_one = lax.psum_scatter(
        grad_normed_one_part.astype(jnp.bfloat16), "tensor", scatter_dimension=0, tiled=True
    ).astype(jnp.float32)
    _, norm_back_one = jax.vjp(layer_norm, block_input, gain_one_f, shift_one_f)
    grad_input_norm, grad_gain_one, grad_shift_one = norm_back_one(grad_normed_one)
    input_grad = grad_resid + grad_input_norm
    query_grad, key_grad, value_grad, output_grad, gain_one_share, shift_one_share = (
        lax.psum_scatter(grad_project[:, :columns], "dp", scatter_dimension=0, tiled=True),
        lax.psum_scatter(
            grad_project[:, columns : 2 * columns], "dp", scatter_dimension=0, tiled=True
        ),
        lax.psum_scatter(grad_project[:, 2 * columns :], "dp", scatter_dimension=0, tiled=True),
        lax.psum_scatter(grad_output_part, "dp", scatter_dimension=1, tiled=True),
        lax.psum_scatter(grad_gain_one, "dp", scatter_dimension=0, tiled=True),
        lax.psum_scatter(grad_shift_one, "dp", scatter_dimension=0, tiled=True),
    )
    first_gain_grad, first_shift_grad, second_gain_grad, second_shift_grad = lax.psum(
        (gain_one_share, shift_one_share, gain_two_share, shift_two_share), "tensor"
    )
    factor = jnp.minimum(1.0, clip_threshold / jnp.maximum(head_maxima, 1.0))
    column_scale = jnp.repeat(jnp.sqrt(factor), HD)
    clipped_query = query_weight * column_scale[None, :]
    clipped_key = key_weight * column_scale[None, :]
    return (
        block_output,
        input_grad,
        query_grad,
        key_grad,
        value_grad,
        output_grad,
        first_gain_grad,
        first_shift_grad,
        expert_in_grad,
        expert_out_grad,
        second_gain_grad,
        second_shift_grad,
        clipped_query,
        clipped_key,
        head_maxima,
    )


def solution(mesh):
    placed = (
        P(("dp", "tensor"), None),
        P(("dp", "tensor"), None),
        P("dp", "tensor"),
        P("dp", "tensor"),
        P("dp", "tensor"),
        P("tensor", "dp"),
        P("dp"),
        P("dp"),
        P(None, "dp", "tensor"),
        P(None, "tensor", "dp"),
        P("dp"),
        P("dp"),
        P("dp", None),
        P("dp", None),
        P("tensor"),
    )
    return jax.shard_map(
        body,
        mesh=mesh,
        in_specs=placed,
        out_specs=(
            P(("dp", "tensor"), None),
            P(("dp", "tensor"), None),
            P("dp", "tensor"),
            P("dp", "tensor"),
            P("dp", "tensor"),
            P("tensor", "dp"),
            P("dp"),
            P("dp"),
            P(None, "dp", "tensor"),
            P(None, "tensor", "dp"),
            P("dp"),
            P("dp"),
            P("dp", "tensor"),
            P("dp", "tensor"),
            P("tensor"),
        ),
        check_vma=False,
    )
```

profile of v0, /device:TPU:0, one launch (start us, length us, event | category | flops | bytes accessed | tf_op | source)
XLA Modules:
  0.0 1848.9 jit_solution(4844986266366260421)
XLA Ops:
  12.8 23.3 %all-reduce.19 = (bf16[768]{0:T(1024)(128)(2,1)S(1)}, bf16[768]{0:T(1024)(128)(2,1)S(1)}, bf16[768]{0:T(1024)(128)(2,1)S(1)}, bf16[768]{0:T(1024)(128)(2,1)S(1)}) all-reduce(bf16[768]{0:T(1024)(128)(2,1)S(1)} %dynamic-update-slice.1, bf16[768]{0:T(1024)(128)(2,1)S(1)} %dynamic-update-slice, ...), channel_id=1, replica_groups=mesh['dp'=8,'tensor'=4] {'dp'}, use_global_device_ids=true, to_apply=%add.2 | all-reduce | flops 3072 | bytes 12288
  43.9 31.0 %all_gather.45 = bf16[768,192]{1,0:T(8,128)(2,1)S(1)} all-gather(bf16[96,192]{1,0:T(8,128)(2,1)S(1)} %convert_element_type.124), channel_id=1, replica_groups=mesh['dp'=8,'tensor'=4] {'dp'}, dimensions={0}, use_global_device_ids=true | all-gather | bytes 331776 | tf_op jit(solution)/shard_map/all_gather | solution.py:109
  74.9 31.2 %all_gather.46 = bf16[768,192]{1,0:T(8,128)(2,1)S(1)} all-gather(bf16[96,192]{1,0:T(8,128)(2,1)S(1)} %convert_element_type.125), channel_id=1, replica_groups=mesh['dp'=8,'tensor'=4] {'dp'}, dimensions={0}, use_global_device_ids=true | all-gather | bytes 331776 | tf_op jit(solution)/shard_map/all_gather | solution.py:110
  106.1 31.1 %all_gather.47 = bf16[768,192]{1,0:T(8,128)(2,1)S(1)} all-gather(bf16[96,192]{1,0:T(8,128)(2,1)S(1)} %convert_element_type.126), channel_id=1, replica_groups=mesh['dp'=8,'tensor'=4] {'dp'}, dimensions={0}, use_global_device_ids=true | all-gather | bytes 331776 | tf_op jit(solution)/shard_map/all_gather | solution.py:111
  137.3 33.0 %all_gather.48 = bf16[192,768]{0,1:T(8,128)(2,1)} all-gather(bf16[192,96]{0,1:T(8,128)(2,1)S(1)} %copy.75), channel_id=1, replica_groups=mesh['dp'=8,'tensor'=4] {'dp'}, dimensions={1}, use_global_device_ids=true | all-gather | bytes 331776 | tf_op jit(solution)/shard_map/all_gather | solution.py:112
  214.6 35.9 %fusion = bf16[592,768]{1,0:T(8,128)(2,1)} fusion(bf16[2364,768]{1,0:T(8,128)(2,1)} %convolution_convert_fusion.1), kind=kCustom, calls=%all-reduce-scatter | all-reduce-scatter fusion | flops 1818625 | bytes 4540928
  271.9 22.9 %scatter_custom_fusion = s32[6336]{0:T(1024)S(1)} fusion(s32[4728]{0:T(1024)S(1)} %fusion.54, s32[4728]{0:T(1024)S(1)} %add_select_fusion, s32[]{:T(128)} %constant.31.clone.1), kind=kCustom, calls=%fused_computation.128 | custom fusion | bytes 25348 | tf_op jit(solution)/shard_map/scatter | solution.py:55
  294.9 22.9 %scatter_custom_fusion.1 = f32[6336]{0:T(1024)S(1)} fusion(s32[4728]{0:T(1024)S(1)} %fusion.54, f32[4728]{0:T(1024)S(1)} %reshape.267, f32[]{:T(128)} %constant.26.clone.1), kind=kCustom, calls=%fused_computation.126 | custom fusion | bytes 25348 | tf_op jit(solution)/shard_map/scatter | solution.py:59
  324.0 26.8 %gather_fusion.2 = bf16[6336,768]{1,0:T(8,128)(2,1)} fusion(bf16[2364,768]{1,0:T(8,128)(2,1)} %reshape.292, s32[7168]{0:T(1024)S(1)} %pad_clamp_fusion), kind=kCustom, calls=%fused_computation.2.clone | custom fusion | bytes 19489536 | tf_op jit(solution)/shard_map/jit(_take)/gather | solution.py:153
  367.2 26.4 %gather_fusion = bf16[6336,768]{1,0:T(8,128)(2,1)} fusion(bf16[2364,768]{1,0:T(8,128)(2,1)} %reshape.290, s32[7168]{0:T(1024)S(1)} %pad_clamp_fusion), kind=kCustom, calls=%fused_computation.clone | custom fusion | bytes 19489536 | tf_op jit(solution)/shard_map/jit(_take)/gather | solution.py:151
  404.3 28.3 %all-gather.11.cloned.1.call-done = bf16[8,768,768]{2,1,0:T(8,128)(2,1)} async-done(((bf16[8,96,768]{2,1,0:T(8,128)(2,1)}), bf16[8,768,768]{2,1,0:T(8,128)(2,1)}) %all-gather.11.cloned.1.call-update) | async-done | bytes 9437200 | tf_op jit(solution)/shard_map/all_gather | solution.py:33
  432.6 21.8 %fusion.13 = (u8[792,768]{1,0:T(8,128)(4,1)S(1)}, u8[792,768]{1,0:T(8,128)(4,1)S(1)}, f32[8,792,768]{2,1,0:T(8,128)}) fusion(bf16[8,792,768]{2,1,0:T(8,128)(2,1)} %bitcast.93, bf16[8,768,768]{2,1,0:T(8,128)(2,1)} %all-gather.11.cloned.1.call-done), kind=kOutput, calls=%fused_computation.42 | convolution fusion | flops 7536291840 | bytes 39849984 | tf_op jit(solution)/shard_map/ecd,edf->ecf/dot_general | solution.py:65
  454.4 116.5 %all-gather.13.cloned.1.call-done = bf16[8,768,768]{1,2,0:T(8,128)(2,1)} async-done(((bf16[8,768,96]{1,2,0:T(8,128)(2,1)}), bf16[8,768,768]{1,2,0:T(8,128)(2,1)}) %all-gather.13.cloned.1.call-update) | async-done | bytes 9437200 | tf_op jit(solution)/shard_map/all_gather | solution.py:34
  570.9 59.4 %add_convert_fusion = (bf16[8,792,768]{2,1,0:T(8,128)(2,1)}, f32[8,792,768]{2,1,0:T(8,128)S(1)}) fusion(f32[8,792,768]{2,1,0:T(8,128)} %get-tuple-element.110, u8[792,768]{1,0:T(8,128)(4,1)S(1)} %get-tuple-element.63, u8[792,768]{1,0:T(8,128)(4,1)S(1)} %get-tuple-element.62, bf16[8,792,768]{2,1,0:T(8,128)(2,1)} %bitcast.95, ...), kind=kOutput, calls=%fused_computation.13 | convolution fusion | flops 7848935424 | bytes 69046272 | tf_op jit(solution)/shard_map/ecd,efd->ecf/dot_general | solution.py:71
  643.3 17.0 fusion.73
  660.3 24.8 %gather_fusion.1 = f32[4728,768]{1,0:T(8,128)} fusion(f32[6336,768]{1,0:T(8,128)} %bitcast.90, s32[5120]{0:T(1024)S(1)} %copy-done.41), kind=kCustom, calls=%fused_computation.1.clone | custom fusion | bytes 29067744 | tf_op jit(solution)/shard_map/jit(_take)/gather | solution.py:158
  685.2 17.4 fusion.74
  702.6 24.9 %gather_fusion.3 = f32[4728,768]{1,0:T(8,128)} fusion(f32[6336,768]{1,0:T(8,128)} %bitcast.89, s32[5120]{0:T(1024)S(1)} %copy-done.41), kind=kCustom, calls=%fused_computation.3.clone | custom fusion | bytes 29067744 | tf_op jit(solution)/shard_map/jit(_take)/gather | solution.py:166
  727.4 18.5 %broadcast_select_fusion.1 = (f32[4728,768]{1,0:T(8,128)}, f32[4728,768]{1,0:T(8,128)}) fusion(f32[4728,768]{1,0:T(8,128)} %gather_fusion.3, pred[4728]{0:T(1024)(128)(4,1)S(1)} %copy-done.61, f32[4728,768]{1,0:T(8,128)} %gather_fusion.1), kind=kLoop, calls=%fused_computation.35 | loop fusion | flops 7262208 | bytes 58102392 | tf_op jit(solution)/shard_map/jit(_take)/select_n | solution.py:166
  745.9 17.2 reshape.217
  763.2 61.3 %reduce_sum.167 = bf16[2364,768]{1,0:T(8,128)(2,1)} reduce(f32[2364,2,768]{2,1,0:T(2,128)} %reshape.217, f32[]{:T(128)} %constant.26.clone.1), dimensions={1}, to_apply=%region_14.17 | reduce | flops 1815552 | bytes 18155524 | tf_op jit(solution)/shard_map/reduce_sum | solution.py:165
  824.5 35.8 %fusion.2 = bf16[592,768]{1,0:T(8,128)(2,1)S(1)} fusion(bf16[2364,768]{1,0:T(8,128)(2,1)} %reduce_sum.167), kind=kCustom, calls=%all-reduce-scatter.2 | all-reduce-scatter fusion | flops 1818625 | bytes 4540928
  871.6 32.0 %all-gather.21.cloned.1.call-done = bf16[4,591,768]{2,1,0:T(8,128)(2,1)} async-done(((bf16[1,591,768]{2,1,0:T(8,128)(2,1)}), bf16[4,591,768]{2,1,0:T(8,128)(2,1)}) %all-gather.21.cloned.1.call-update) | async-done | bytes 3631120 | tf_op jit(solution)/shard_map/all_gather | solution.py:184
  960.3 19.4 %fusion.77 = f32[8,768,768]{1,2,0:T(8,128)} fusion(bf16[8,792,768]{2,1,0:T(8,128)(2,1)} %multiply_convert_fusion.1, bf16[8,792,768]{2,1,0:T(8,128)(2,1)} %bitcast.96), kind=kOutput, calls=%fused_computation.160 | convolution fusion | flops 7474249728 | bytes 38338560 | tf_op jit(solution)/shard_map/ecf,ecd->efd/dot_general | solution.py:70
  979.8 19.3 %fusion.76 = f32[8,768,768]{2,1,0:T(8,128)} fusion(bf16[8,792,768]{2,1,0:T(8,128)(2,1)} %bitcast.94, bf16[8,792,768]{2,1,0:T(8,128)(2,1)} %get-tuple-element.90), kind=kOutput, calls=%fused_computation.159 | convolution fusion | flops 7474249728 | bytes 38338560 | tf_op jit(solution)/shard_map/ecd,ecf->edf/dot_general | solution.py:74
  999.8 21.6 %pmax.7 = f32[3]{0:T(128)S(1)} all-reduce(f32[3]{0:T(128)S(1)} %copy-done.64), channel_id=1, replica_groups=mesh['dp'=8,'tensor'=4] {'dp'}, use_global_device_ids=true, to_apply=%region_41.44 | all-reduce | flops 3 | bytes 24 | tf_op jit(solution)/shard_map/pmax | solution.py:141
  1021.6 17.4 reshape.213
  1039.0 22.6 %multiply_reduce_fusion = bf16[2364,768]{1,0:T(8,128)(2,1)} fusion(f32[2364,2,768]{2,1,0:T(2,128)} %reshape.213, f32[2364,2]{1,0:T(8,128)S(1)} %copy-done.11), kind=kLoop, calls=%fused_computation.28 | loop fusion | flops 5446656 | bytes 18174432 | tf_op jit(solution)/shard_map/reduce_sum | solution.py:161
  1068.4 65.2 %fusion.66 = (bf16[592,768]{1,0:T(8,128)(2,1)S(1)}, bf16[592,768]{1,0:T(8,128)(2,1)}) fusion(bf16[2364,768]{1,0:T(8,128)(2,1)} %multiply_reduce_fusion, bf16[2364,768]{1,0:T(8,128)(2,1)} %convolution_convert_fusion), kind=kCustom, calls=%all-reduce-scatter.4 | all-reduce-scatter fusion | flops 3637249 | bytes 9081344
  1146.9 33.1 %all-reduce.17 = (f32[768]{0:T(1024)S(1)}, f32[768]{0:T(1024)S(1)}, f32[768]{0:T(1024)S(1)}, f32[768]{0:T(1024)S(1)}) all-reduce(f32[768]{0:T(1024)S(1)} %get-tuple-element.66, f32[768]{0:T(1024)S(1)} %get-tuple-element.71, f32[768]{0:T(1024)S(1)} %get-tuple-element.68, ...), channel_id=10, replica_groups=mesh['dp'=8,'tensor'=4] {'dp'}, use_global_device_ids=true, to_apply=%region_27.30.clone | all-reduce | flops 3072 | bytes 24576
  1208.3 316.8 %reduce-scatter.25.cloned.1.call-done = f32[8,768,96]{1,2,0:T(8,128)} async-done(((f32[8,768,768]{1,2,0:T(8,128)}), f32[8,768,96]{1,2,0:T(8,128)}) %reduce-scatter.25.cloned.1.call-update) | async-done | bytes 2359312 | tf_op jit(solution)/shard_map/reduce_scatter | solution.py:179
  1525.0 316.8 %reduce-scatter.23.cloned.1.call-done = f32[8,96,768]{2,1,0:T(8,128)} async-done(((f32[8,768,768]{2,1,0:T(8,128)}), f32[8,96,768]{2,1,0:T(8,128)}) %reduce-scatter.23.cloned.1.call-update) | async-done | bytes 2359312 | tf_op jit(solution)/shard_map/reduce_scatter | solution.py:178
  (307 shorter events, 239.6 us)
Async XLA Ops:
  7.2 163.1 %all-gather.15.cloned.1.call-start = ((), (), s32[]{:S(2)}) async-start(), calls=%async_computation.10 | async-start | bytes 4546560 | tf_op jit(solution)/shard_map/all_gather | solution.py:119
  37.9 68.2 %copy-start.48 = (f32[96,192]{1,0:T(8,128)S(1)}, f32[96,192]{1,0:T(8,128)}, u32[]{:S(2)}) copy-start(f32[96,192]{1,0:T(8,128)} %param.23) | copy-start | bytes 221188
  39.8 97.4 %copy-start.49 = (f32[192,96]{1,0:T(8,128)S(1)}, f32[192,96]{1,0:T(8,128)}, u32[]{:S(2)}) copy-start(f32[192,96]{1,0:T(8,128)} %param.24) | copy-start | bytes 221188
  41.2 277.9 %all-gather.19.cloned.1.call-start = ((), (), s32[]{:S(2)}) async-start(), calls=%async_computation.12 | async-start | bytes 4546560 | tf_op jit(solution)/shard_map/all_gather | solution.py:149
  43.8 318.6 %all-gather.17.cloned.1.call-start = ((), (), s32[]{:S(2)}) async-start(), calls=%async_computation.11 | async-start | bytes 4546560 | tf_op jit(solution)/shard_map/all_gather | solution.py:148
  74.9 104.8 %copy-start.29 = (bf16[768,192]{1,0:T(8,128)(2,1)}, bf16[768,192]{1,0:T(8,128)(2,1)S(1)}, u32[]{:S(2)}) copy-start(bf16[768,192]{1,0:T(8,128)(2,1)S(1)} %all_gather.45) | copy-start | bytes 884740
  106.1 73.7 %copy-start.31 = (bf16[768,192]{1,0:T(8,128)(2,1)}, bf16[768,192]{1,0:T(8,128)(2,1)S(1)}, u32[]{:S(2)}) copy-start(bf16[768,192]{1,0:T(8,128)(2,1)S(1)} %all_gather.46) | copy-start | bytes 884740
  251.2 2.5 collective-permute-start
  261.3 171.3 %all-gather.11.cloned.1.call-start = ((), (), s32[]{:S(2)}) async-start(), calls=%async_computation.6 | async-start | bytes 10616832 | tf_op jit(solution)/shard_map/all_gather | solution.py:33
  262.6 308.3 %all-gather.13.cloned.1.call-start = ((), (), s32[]{:S(2)}) async-start(), calls=%async_computation.7 | async-start | bytes 10616832 | tf_op jit(solution)/shard_map/all_gather | solution.py:34
  265.5 638.1 %all-gather.21.cloned.1.call-start = ((), (), s32[]{:S(2)}) async-start(), calls=%async_computation.13 | async-start | bytes 4546560 | tf_op jit(solution)/shard_map/all_gather | solution.py:184
  271.2 79.6 %copy-start.10 = (f32[2364,2]{1,0:T(8,128)}, f32[2364,2]{1,0:T(8,128)S(1)}, u32[]{:S(2)}) copy-start(f32[2364,2]{1,0:T(8,128)S(1)} %copy.79) | copy-start | bytes 56740
  824.5 42.7 %copy-start.47 = (f32[591]{0:T(1024)S(1)}, f32[591]{0:T(1024)}, u32[]{:S(2)}) copy-start(f32[591]{0:T(1024)} %copy-done.46) | copy-start | bytes 7096
  824.5 42.7 %copy-start.54 = (f32[768]{0:T(1024)S(1)}, f32[768]{0:T(1024)}, u32[]{:S(2)}) copy-start(f32[768]{0:T(1024)} %copy-done.53) | copy-start | bytes 9220
  824.5 42.7 %copy-start.56 = (f32[591]{0:T(1024)S(1)}, f32[591]{0:T(1024)}, u32[]{:S(2)}) copy-start(f32[591]{0:T(1024)} %copy-done.55) | copy-start | bytes 7096
  824.5 43.7 %copy-start.60 = (f32[591]{0:T(1024)S(1)}, f32[591]{0:T(1024)}, u32[]{:S(2)}) copy-start(f32[591]{0:T(1024)} %copy-done.59) | copy-start | bytes 7096
  860.3 2.1 collective-permute-start.2
  871.5 326.5 %reduce-scatter.33.cloned.1.call-start = ((), (), s32[]{:S(2)}) async-start(), calls=%async_computation.17 | async-start | bytes 884736
  948.9 250.8 %reduce-scatter.27.cloned.1.call-start = ((), (), s32[]{:S(2)}) async-start(), calls=%async_computation.14 | async-start | bytes 884736
  957.7 241.9 %reduce-scatter.29.cloned.1.call-start = ((), (), s32[]{:S(2)}) async-start(), calls=%async_computation.15 | async-start | bytes 884736
  959.0 249.3 %reduce-scatter.31.cloned.1.call-start = ((), (), s32[]{:S(2)}) async-start(), calls=%async_computation.16 | async-start | bytes 884736
  960.3 564.8 %reduce-scatter.25.cloned.1.call-start = ((), (), s32[]{:S(2)}) async-start(), calls=%async_computation.9 | async-start | bytes 21233664 | tf_op jit(solution)/shard_map/reduce_scatter | solution.py:179
  979.8 862.1 %reduce-scatter.23.cloned.1.call-start = ((), (), s32[]{:S(2)}) async-start(), calls=%async_computation.8 | async-start | bytes 21233664 | tf_op jit(solution)/shard_map/reduce_scatter | solution.py:178
  1068.4 67.2 %copy-start.36 = (f32[96,192]{1,0:T(8,128)S(1)}, f32[96,192]{1,0:T(8,128)}, u32[]{:S(2)}) copy-start(f32[96,192]{1,0:T(8,128)} %param.22) | copy-start | bytes 221188
  1068.4 67.2 %copy-start.38 = (f32[96,192]{1,0:T(8,128)S(1)}, f32[96,192]{1,0:T(8,128)}, u32[]{:S(2)}) copy-start(f32[96,192]{1,0:T(8,128)} %param.21) | copy-start | bytes 221188
  1068.4 76.6 %copy-start.2 = (f32[591,768]{1,0:T(8,128)S(1)}, f32[591,768]{1,0:T(8,128)}, u32[]{:S(2)}) copy-start(f32[591,768]{1,0:T(8,128)} %param.19) | copy-start | bytes 5446660
  1068.4 76.6 %copy-start.43 = (f32[591]{0:T(1024)S(1)}, f32[591]{0:T(1024)}, u32[]{:S(2)}) copy-start(f32[591]{0:T(1024)} %copy-done.42) | copy-start | bytes 7096
  1068.4 76.6 %copy-start.45 = (f32[768]{0:T(1024)S(1)}, f32[768]{0:T(1024)}, u32[]{:S(2)}) copy-start(f32[768]{0:T(1024)} %copy-done.44) | copy-start | bytes 9220
  1068.4 77.4 %copy-start.58 = (f32[591]{0:T(1024)S(1)}, f32[591]{0:T(1024)}, u32[]{:S(2)}) copy-start(f32[591]{0:T(1024)} %copy-done.57) | copy-start | bytes 7096
  1068.4 77.4 %copy-start.52 = (f32[591]{0:T(1024)S(1)}, f32[591]{0:T(1024)}, u32[]{:S(2)}) copy-start(f32[591]{0:T(1024)} %copy-done.51) | copy-start | bytes 7096
  1134.3 6.1 collective-permute-start.3
  1136.3 44.0 %collective-permute-start.1 = (bf16[3,768]{1,0:T(4,128)(2,1)S(1)}, bf16[3,768]{1,0:T(4,128)(2,1)S(1)}, u32[]{:S(2)}, u32[]{:S(2)}) collective-permute-start(bf16[3,768]{1,0:T(4,128)(2,1)S(1)} %slice.53), channel_id=1, source_target_pairs={{0,1},{1,2},{2,3},{4,5},{5,6},{6,7},{8,9},{9,10},{10,11},{12,13},{... | collective-permute-start | bytes 13832
  (53 other events, 610.4 us)
Sparse Core Ops, SparseCore 0:
  41.3 28.5 all-gather.14
  71.5 31.3 all-gather.18
  261.4 30.9 all-gather.16
  294.5 138.0 all-gather.10
  434.6 136.2 all-gather.12
  871.6 31.9 all-gather.20
  949.0 62.5 reduce-scatter.32
  1015.8 61.4 reduce-scatter.26
  1081.2 61.4 reduce-scatter.28
  1146.7 61.5 reduce-scatter.30
  1212.7 312.2 reduce-scatter.24
  1529.4 312.4 reduce-scatter.22
where the time goes:
time: 1860 us; the launch traced here: 1850 us
  waiting for transfers between devices  820 us (44%)
  blocking collectives  347 us (19%)
  local copies, waits for them, and re-layouts  281 us (15%)
  matrix products  201 us (11%)
  other arithmetic  174 us (9%)
    reduce_scatter x1, waiting for transfers between devices, body(): lax.psum_scatter(grad_up, 'dp', scatter_dimension=1, tiled=True)  317 us
    reduce_scatter x1, waiting for transfers between devices, body(): lax.psum_scatter(grad_down, 'dp', scatter_dimension=2, tiled=True)  317 us
    unnamed x5, blocking collectives  193 us
    all_gather x1, waiting for transfers between devices, expert_params(): lax.all_gather(to_half(expert_out), 'dp', axis=2, tiled=True)  117 us
    reduce_sum x1, other arithmetic, body(): jnp.sum(jnp.take(grad_slots.reshape(experts * CAP, features), slot_of_rou...  61.3 us
    dot_general x1, matrix products, expert_math(): jnp.einsum('ecd,efd->ecf', slot_cot, weight_out, preferred_element_type=j...  59.4 us
    unnamed x174, local copies, waits for them, and re-layouts  55.3 us
  transfers between devices with their start and end apart: 16, of which 7 were waited for; matrix products, arithmetic and copies ran while one was open for 24% of the time, Pallas kernels for 0%

commit v1 on v0

v1 whole, which is shorter than its diff:
```python
import functools
import math

import jax
import jax.numpy as jnp
from jax import lax
from jax.experimental import pallas as pl
from jax.experimental.pallas import tpu as pltpu
from jax.sharding import PartitionSpec as P

HD = 64
SEQ = 197
CAP = 792
EPSILON = 1e-06
F32 = jnp.float32
BF16 = jnp.bfloat16
OUTER = 8
EXTRA = 16
ROW_TILE = 400
WINDOW = 256
MIB = 1 << 20


def up(number, unit):
    return -(-number // unit) * unit


def dot(left, right, contract=((1,), (0,))):
    return lax.dot_general(left, right, (contract, ((), ())), preferred_element_type=F32)


def params(mib):
    return pltpu.CompilerParams(vmem_limit_bytes=mib * MIB)


def any_spec():
    return pl.BlockSpec(memory_space=pl.ANY)


def vmem_spec():
    return pl.BlockSpec(memory_space=pltpu.VMEM)


def smem_spec():
    return pl.BlockSpec(memory_space=pltpu.SMEM)


def sds(shape, dtype):
    return jax.ShapeDtypeStruct(shape, dtype)


def cost(flops, moved, trans=0):
    return pl.CostEstimate(flops=int(flops), bytes_accessed=int(moved), transcendentals=int(trans))


def block_flip(x_bit, low_bit, high_bit):
    return x_bit | low_bit << 1 | high_bit << 2


def norm_stats(values):
    mean = jnp.mean(values, -1, keepdims=True)
    centred = values - mean
    scale = lax.rsqrt(jnp.mean(centred * centred, -1, keepdims=True) + EPSILON)
    return centred * scale, scale


def spread_rows(source, target, images, stride):
    for i in range(images):
        target[i * stride : i * stride + SEQ, :] = source[i * SEQ : (i + 1) * SEQ, :].astype(F32)
        end = (i + 1) * stride if i + 1 < images else target.shape[0]
        target[i * stride + SEQ : end, :] = jnp.zeros((end - i * stride - SEQ, target.shape[1]), F32)


def gather_rows(source, target, images, stride):
    for i in range(images):
        target[i * SEQ : (i + 1) * SEQ, :] = source[i * stride : i * stride + SEQ, :]


def attention_forward_kernel(images, stride, heads, layout, *refs):
    n_pieces = len(layout)
    place_ref, x_ref, gains_ref = refs[:3]
    piece_refs = refs[3 : 3 + n_pieces]
    res_ref, second_ref, first_ref, w_ref, kept_ref, peak_ref = refs[3 + n_pieces : 9 + n_pieces]
    scratch, sems = refs[9 + n_pieces :]
    columns = heads * HD
    block = w_ref.shape[1] // OUTER
    place = place_ref[0]
    copies = []
    for ref, entries in zip(piece_refs, layout):
        for j, (t, flip) in enumerate(entries):
            row = pl.multiple_of((place ^ flip) * block, 16)
            copies.append(
                pltpu.make_async_copy(
                    ref.at[j, pl.ds(0, block), :],
                    w_ref.at[t, pl.ds(row, block), :],
                    sems.at[len(copies)],
                )
            )
            copies[-1].start()
    spread_rows(x_ref, res_ref, images, stride)
    unit, _ = norm_stats(res_ref[...])
    first_ref[...] = (unit * gains_ref[0:1, :] + gains_ref[1:2, :]).astype(BF16)
    for copy in copies:
        copy.wait()
    scale = 1.0 / math.sqrt(HD)
    col_ok = lax.broadcasted_iota(jnp.int32, (stride, stride), 1) < SEQ
    row_ok = lax.broadcasted_iota(jnp.int32, (stride, 1), 0) < SEQ
    lane = lax.broadcasted_iota(jnp.int32, (8, 128), 1)

    def step(t, carry):
        scratch[...] = dot(first_ref[...], w_ref[t]).astype(BF16).astype(F32)
        peaks = jnp.full((8, 128), -jnp.inf, F32)
        for i in range(images):
            rows = slice(i * stride, (i + 1) * stride)
            for h in range(heads):
                at = [slice((1 + p) * columns + h * HD, (1 + p) * columns + (h + 1) * HD) for p in range(3)]
                q = (scratch[rows, at[0]] * scale).astype(BF16)
                k = scratch[rows, at[1]].astype(BF16)
                v = scratch[rows, at[2]].astype(BF16)
                s = jnp.where(col_ok, dot(q, k, ((1,), (1,))), -1e30)
                top = jnp.max(s, -1, keepdims=True)
                e = jnp.exp(s - top)
                p = e * (1.0 / jnp.sum(e, -1, keepdims=True))
                o = dot(p.astype(BF16), v)
                scratch[rows, h * HD : (h + 1) * HD] = o.astype(BF16).astype(F32)
                peak = jnp.max(jnp.where(row_ok, top, -jnp.inf), keepdims=True)
                peaks = jnp.maximum(peaks, jnp.where(lane == h, peak, -jnp.inf))
        peak_ref[t] = peaks
        kept_ref[t] = scratch[...].astype(BF16)
        res_ref[...] += dot(kept_ref[t, :, 0:columns], w_ref[t, :, 0:columns], ((1,), (1,)))
        return carry

    lax.fori_loop(0, w_ref.shape[0], step, 0)
    unit, _ = norm_stats(res_ref[...])
    second_ref[...] = (unit * gains_ref[2:3, :] + gains_ref[3:4, :]).astype(BF16)


def attention_forward(place, rows, gains, pieces, layout, images, stride, padded, parts, heads):
    features = rows.shape[1]
    n_copies = sum(len(entries) for entries in layout)
    return pl.pallas_call(
        functools.partial(attention_forward_kernel, images, stride, heads, layout),
        out_shape=(
            sds((padded, features), F32),
            sds((padded, features), BF16),
            sds((padded, features), BF16),
            sds((parts, features, features), BF16),
            sds((parts, padded, features), BF16),
            sds((parts, 8, 128), F32),
        ),
        in_specs=[smem_spec(), vmem_spec(), vmem_spec()] + [any_spec()] * len(pieces),
        out_specs=(vmem_spec(),) * 6,
        scratch_shapes=[
            pltpu.VMEM((padded, features), F32),
            pltpu.SemaphoreType.DMA((n_copies,)),
        ],
        compiler_params=params(48),
        cost_estimate=cost(parts * padded * features * features * 2.6 * 4, 20e6, 2e6),
        name="attention_forward",
    )(place, rows, gains, *pieces)


def attention_backward_kernel(images, stride, heads, *refs):
    (x_ref, cot_ref, res_ref, d0_ref, d1_ref, d2_ref, first_ref, w_ref, kept_ref, gains_ref, extra_ref) = refs[:11]
    input_grad_ref, keep_ref, send_ref = refs[11:14]
    resid, total, kept, grads, mixed, half = refs[14:]
    columns = heads * HD
    parts = w_ref.shape[0]
    features = w_ref.shape[1]
    block = features // OUTER
    unit, scale_two = norm_stats(res_ref[...])
    da2 = d0_ref[...].astype(F32) + d1_ref[...].astype(F32) + d2_ref[...].astype(F32)
    gain_two = jnp.sum(da2 * unit, 0, keepdims=True)
    shift_two = jnp.sum(da2, 0, keepdims=True)
    weighted = da2 * gains_ref[2:3, :]
    back = (
        weighted
        - jnp.mean(weighted, -1, keepdims=True)
        - unit * jnp.mean(weighted * unit, -1, keepdims=True)
    ) * scale_two
    spread_rows(cot_ref, resid, images, stride)
    resid[...] += back
    half[...] = resid[...].astype(BF16)
    total[...] = jnp.zeros_like(total)
    grads[...] = jnp.zeros_like(grads)
    scale = 1.0 / math.sqrt(HD)
    col_ok = lax.broadcasted_iota(jnp.int32, (stride, stride), 1) < SEQ

    def step(t, carry):
        kept[...] = kept_ref[t].astype(F32)
        mixed[...] = dot(half[...], w_ref[t, :, 0:columns]).astype(BF16).astype(F32)
        for i in range(images):
            rows = slice(i * stride, (i + 1) * stride)
            for h in range(heads):
                at = [slice((1 + p) * columns + h * HD, (1 + p) * columns + (h + 1) * HD) for p in range(3)]
                q = (kept[rows, at[0]] * scale).astype(BF16)
                k = kept[rows, at[1]].astype(BF16)
                v = kept[rows, at[2]].astype(BF16)
                do = mixed[rows, h * HD : (h + 1) * HD].astype(BF16)
                s = jnp.where(col_ok, dot(q, k, ((1,), (1,))), -1e30)
                e = jnp.exp(s - jnp.max(s, -1, keepdims=True))
                p = e * (1.0 / jnp.sum(e, -1, keepdims=True))
                dp = dot(do, v, ((1,), (1,)))
                dv = dot(p.astype(BF16), do, ((0,), (0,)))
                ds = (p * (dp - jnp.sum(p * dp, -1, keepdims=True))).astype(BF16)
                dq = dot(ds, k) * scale
                dk = dot(ds, q, ((0,), (0,)))
                grads[rows, at[0]] = dq
                grads[rows, at[1]] = dk
                grads[rows, at[2]] = dv
        packed = grads[...].astype(BF16)
        total[...] += dot(packed, w_ref[t], ((1,), (1,)))
        full = dot(first_ref[...], packed, ((0,), (0,)))
        out = dot(half[...], kept_ref[t, :, 0:columns], ((0,), (0,)))
        full = full + jnp.concatenate((out, jnp.zeros((features, features - columns), F32)), 1)
        full = full.astype(BF16)

        def put(ref, index):
            for j in range(OUTER):
                ref[index, j, 0:block, :] = full[j * block : (j + 1) * block, :]

        @pl.when(t < parts // 2)
        def _():
            put(keep_ref, t)

        @pl.when(t >= parts // 2)
        def _():
            put(send_ref, t - parts // 2)

        return carry

    lax.fori_loop(0, parts, step, 0)
    spread_rows(x_ref, kept, images, stride)
    unit, scale_one = norm_stats(kept[...])
    da = total[...]
    gain_one = jnp.sum(da * unit, 0, keepdims=True)
    shift_one = jnp.sum(da, 0, keepdims=True)
    weighted = da * gains_ref[0:1, :]
    back = (
        weighted
        - jnp.mean(weighted, -1, keepdims=True)
        - unit * jnp.mean(weighted * unit, -1, keepdims=True)
    ) * scale_one
    resid[...] += back
    gather_rows(resid, input_grad_ref, images, stride)
    row = lax.broadcasted_iota(jnp.int32, (EXTRA, features), 0)
    extra = extra_ref[...]
    for number, value in enumerate((gain_one, shift_one, gain_two, shift_two)):
        extra = jnp.where(row == number, value, extra)
    extra = extra.astype(BF16)
    for ref in (keep_ref, send_ref):
        for t in range(parts // 2):
            for j in range(OUTER):
                ref[t, j, block : block + EXTRA, :] = extra


def attention_backward(rows, cot, residual, pieces, first, weights, kept, gains, extra, images, stride, heads):
    padded, features = first.shape
    parts = weights.shape[0]
    share = sds((parts // 2, OUTER, features // OUTER + EXTRA, features), BF16)
    return pl.pallas_call(
        functools.partial(attention_backward_kernel, images, stride, heads),
        out_shape=(sds(rows.shape, F32), share, share),
        in_specs=[vmem_spec()] * 11,
        out_specs=(vmem_spec(),) * 3,
        scratch_shapes=[
            pltpu.VMEM((padded, features), F32),
            pltpu.VMEM((padded, features), F32),
            pltpu.VMEM((padded, features), F32),
            pltpu.VMEM((padded, features), F32),
            pltpu.VMEM((padded, heads * HD), F32),
            pltpu.VMEM((padded, features), BF16),
        ],
        compiler_params=params(56),
        cost_estimate=cost(parts * padded * features * features * 2 * 4, 30e6, 2e6),
        name="attention_backward",
    )(rows, cot, residual, *pieces, first, weights, kept, gains, extra)


def dispatch_kernel(gated, *refs):
    table_ref = refs[0]
    n_shards = 8
    shard_refs = refs[1 : 1 + n_shards]
    slot_ref = refs[1 + n_shards]
    gate_ref = refs[2 + n_shards] if gated else None
    out_ref = refs[-1]
    expert = pl.program_id(0)
    experts = pl.num_programs(0)
    padded = shard_refs[0].shape[0]
    features = shard_refs[0].shape[1]
    count_all = table_ref[2 * n_shards * experts + expert]
    tail = pl.multiple_of(count_all // 16 * 16, 16)
    out_ref[0, pl.ds(tail, ROW_TILE + 16), :] = jnp.zeros((ROW_TILE + 16, features), BF16)
    row16 = lax.broadcasted_iota(jnp.int32, (16, 1), 0)
    rows = lax.broadcasted_iota(jnp.int32, (WINDOW, padded), 0)
    for r in range(n_shards):
        start = table_ref[expert * n_shards + r]
        number = table_ref[n_shards * experts + expert * n_shards + r]
        first = start // 16 * 16
        steps = jnp.where(number > 0, (start - first + number + WINDOW - 1) // WINDOW, 0)

        def step(c, carry, r=r, start=start, first=first):
            low = pl.multiple_of(first + c * WINDOW, 16)
            hit = slot_ref[0, r : r + 1, :] == rows + low
            chosen = jnp.where(hit, 1.0, 0.0)
            got = dot(chosen.astype(BF16), shard_refs[r][...])
            if gated:
                got = got * jnp.sum(chosen * gate_ref[0, r : r + 1, :], -1, keepdims=True)
            got = got.astype(BF16)
            before = out_ref[0, pl.ds(low, 16), :]
            out_ref[0, pl.ds(low, 16), :] = jnp.where(row16 + low < start, before, got[:16])
            out_ref[0, pl.ds(low + 16, WINDOW - 16), :] = got[16:]
            return carry

        lax.fori_loop(0, steps, step, 0)


def slot_rows(limit):
    return up(limit + ROW_TILE, 16) + up(ROW_TILE, 16)


def dispatch(table, shards, slots, gates, limit):
    experts = slots.shape[0]
    padded, features = shards[0].shape
    length = slot_rows(limit)
    gated = gates is not None
    per_expert = pl.BlockSpec((1,) + slots.shape[1:], lambda e: (e, 0, 0))
    return pl.pallas_call(
        functools.partial(dispatch_kernel, gated),
        grid=(experts,),
        out_shape=sds((experts, length, features), BF16),
        in_specs=[smem_spec()] + [vmem_spec()] * len(shards) + [per_expert] * (2 if gated else 1),
        out_specs=pl.BlockSpec((1, length, features), lambda e: (e, 0, 0)),
        compiler_params=params(48),
        cost_estimate=cost(experts * 8 * WINDOW * padded * features * 2, 20e6),
        name="dispatch_gated" if gated else "dispatch",
    )(table, *shards, slots, *([gates] if gated else []))


def expert_kernel(layout, *refs):
    info_ref, x_ref, dy_ref = refs[:3]
    w_refs = refs[3:11]
    y_ref, dx_ref, keep_ref, send_ref = refs[11:15]
    w_in, w_out, g_in, g_out = refs[15:]
    place = info_ref[0]
    count = info_ref[1 + pl.program_id(0)]
    features = w_in.shape[0]
    block = features // OUTER
    for ref, flip in zip(w_refs, layout):
        row = pl.multiple_of((place ^ flip) * block, 16)
        w_in[pl.ds(row, block), :] = ref[0, 0]
        w_out[pl.ds(row, block), :] = ref[0, 1]
    g_in[...] = jnp.zeros_like(g_in)
    g_out[...] = jnp.zeros_like(g_out)
    tiles = (count + ROW_TILE - 1) // ROW_TILE

    def tile(i, carry):
        rows = pl.ds(pl.multiple_of(i * ROW_TILE, 16), ROW_TILE)
        x = x_ref[0, rows, :]
        dy = dy_ref[0, rows, :]
        pre = dot(x, w_in[...])
        share = 0.5 * (1.0 + lax.erf(pre * (1.0 / math.sqrt(2.0))))
        hid = (pre * share).astype(BF16)
        slope = share + pre * jnp.exp(-0.5 * pre * pre) * (1.0 / math.sqrt(2.0 * math.pi))
        y_ref[0, rows, :] = dot(hid, w_out[...], ((1,), (1,))).astype(BF16)
        dpre = (dot(dy, w_out[...]) * slope).astype(BF16)
        dx_ref[0, rows, :] = dot(dpre, w_in[...], ((1,), (1,))).astype(BF16)
        g_in[...] += dot(x, dpre, ((0,), (0,)))
        g_out[...] += dot(dy, hid, ((0,), (0,)))
        return carry

    lax.fori_loop(0, tiles, tile, 0)
    rest = pl.ds(pl.multiple_of(tiles * ROW_TILE, 16), WINDOW + 16)
    y_ref[0, rest, :] = jnp.zeros((WINDOW + 16, features), BF16)
    dx_ref[0, rest, :] = jnp.zeros((WINDOW + 16, features), BF16)
    for number in range(OUTER):
        flip = block_flip(number >> 2 & 1, number & 1, number >> 1 & 1)
        row = pl.multiple_of((place ^ flip) * block, 16)
        target = send_ref if number >= OUTER // 2 else keep_ref
        at = slice(number % (OUTER // 2) * block, (number % (OUTER // 2) + 1) * block)
        target[0, 0, at, :] = g_in[pl.ds(row, block), :].astype(BF16)
        target[0, 1, at, :] = g_out[pl.ds(row, block), :].astype(BF16)


def expert_math(info, x, dy, weights, layout, first, limit):
    experts = weights[0].shape[0]
    length, features = x.shape[1:]
    hidden = weights[0].shape[3]
    most = up(limit, ROW_TILE)
    slots_spec = pl.BlockSpec((1, most, features), lambda e: (e + first, 0, 0))
    out_spec = pl.BlockSpec((1, length, features), lambda e: (e, 0, 0))
    share = sds((experts, 2, features // 2, hidden), BF16)
    share_spec = pl.BlockSpec((1, 2, features // 2, hidden), lambda e: (e, 0, 0, 0))
    return pl.pallas_call(
        functools.partial(expert_kernel, layout),
        grid=(experts,),
        out_shape=(sds((experts, length, features), BF16),) * 2 + (share,) * 2,
        in_specs=[smem_spec(), slots_spec, slots_spec]
        + [pl.BlockSpec((1,) + w.shape[1:], lambda e: (e, 0, 0, 0)) for w in weights],
        out_specs=(out_spec, out_spec, share_spec, share_spec),
        scratch_shapes=[
            pltpu.VMEM((features, hidden), BF16),
            pltpu.VMEM((features, hidden), BF16),
            pltpu.VMEM((features, hidden), F32),
            pltpu.VMEM((features, hidden), F32),
        ],
        compiler_params=params(60),
        cost_estimate=cost(experts * 12 * limit * features * hidden, 30e6, 4e6),
        name="expert_math",
    )(info, x, dy, *weights)


def combine_kernel(gated, n_sources, *refs):
    table_ref = refs[0]
    source_refs = refs[1 : 1 + n_sources]
    slot_ref = refs[1 + n_sources]
    gate_ref = refs[2 + n_sources] if gated else None
    send_ref, keep_ref, window = refs[-3:]
    r = pl.program_id(0)
    n_shards = pl.num_programs(0)
    per_source = source_refs[0].shape[0]
    experts = per_source * n_sources
    shard = lax.rem(r + n_shards // 2, n_shards)
    padded = slot_ref.shape[1]
    lanes = lax.broadcasted_iota(jnp.int32, (padded, WINDOW), 1)

    def chosen(e, low):
        hit = slot_ref[0, :, e : e + 1] == lanes + low
        return jnp.where(hit, gate_ref[0, :, e : e + 1] if gated else 1.0, 0.0).astype(BF16)

    firsts, steps, parts = [], [], []
    for e in range(experts):
        start = table_ref[e * n_shards + shard]
        number = table_ref[n_shards * experts + e * n_shards + shard]
        first = pl.multiple_of(start // 16 * 16, 16)
        firsts.append(first)
        steps.append((start - first + number + WINDOW - 1) // WINDOW)
        window[e * WINDOW : (e + 1) * WINDOW, :] = source_refs[e // per_source][e % per_source, pl.ds(first, WINDOW), :]
        parts.append(chosen(e, first))
    total = dot(jnp.concatenate(parts, 1), window[...]).astype(BF16)

    def finish(ref):
        ref[0] = total
        for e in range(experts):

            def step(c, carry, e=e):
                low = pl.multiple_of(firsts[e] + c * WINDOW, 16)
                rows = source_refs[e // per_source][e % per_source, pl.ds(low, WINDOW), :]
                ref[0] = (ref[0].astype(F32) + dot(chosen(e, low), rows)).astype(BF16)
                return carry

            lax.fori_loop(1, steps[e], step, 0)

    @pl.when(r < n_shards // 2)
    def _():
        finish(send_ref)

    @pl.when(r >= n_shards // 2)
    def _():
        finish(keep_ref)


def combine(table, sources, slots, gates):
    n_shards, padded, experts = slots.shape
    features = sources[0].shape[2]
    gated = gates is not None
    half = n_shards // 2
    per_shard = pl.BlockSpec((1, padded, experts), lambda r: (lax.rem(r + half, n_shards), 0, 0))
    share = sds((half, padded, features), BF16)
    return pl.pallas_call(
        functools.partial(combine_kernel, gated, len(sources)),
        grid=(n_shards,),
        out_shape=(share, share),
        in_specs=[smem_spec()] + [vmem_spec()] * len(sources) + [per_shard] * (2 if gated else 1),
        out_specs=(
            pl.BlockSpec((1, padded, features), lambda r: (jnp.minimum(r, half - 1), 0, 0)),
            pl.BlockSpec((1, padded, features), lambda r: (jnp.maximum(r - half, 0), 0, 0)),
        ),
        scratch_shapes=[pltpu.VMEM((experts * WINDOW, features), BF16)],
        compiler_params=params(48),
        cost_estimate=cost(n_shards * experts * WINDOW * padded * features * 2, 20e6),
        name="combine_gated" if gated else "combine",
    )(table, *sources, slots, *([gates] if gated else []))


def spread_kernel(images, stride, x_ref, out_ref, scratch):
    spread_rows(x_ref, scratch, images, stride)
    out_ref[...] = scratch[...].astype(BF16)


def spread(rows, images, stride, padded):
    return pl.pallas_call(
        functools.partial(spread_kernel, images, stride),
        out_shape=sds((padded, rows.shape[1]), BF16),
        in_specs=[vmem_spec()],
        out_specs=vmem_spec(),
        scratch_shapes=[pltpu.VMEM((padded, rows.shape[1]), F32)],
        compiler_params=params(16),
        cost_estimate=cost(1e6, 3e6),
        name="spread_rows",
    )(rows)


def finish_kernel(images, stride, res_ref, a_ref, b_ref, c_ref, out_ref, scratch):
    mixture = a_ref[...].astype(F32) + b_ref[...].astype(F32) + c_ref[...].astype(F32)
    scratch[...] = res_ref[...] + mixture
    gather_rows(scratch, out_ref, images, stride)


def finish(residual, pieces, tokens, images, stride):
    return pl.pallas_call(
        functools.partial(finish_kernel, images, stride),
        out_shape=sds((tokens, residual.shape[1]), F32),
        in_specs=[vmem_spec()] * 4,
        out_specs=vmem_spec(),
        scratch_shapes=[pltpu.VMEM(residual.shape, F32)],
        compiler_params=params(24),
        cost_estimate=cost(1e6, 6e6),
        name="finish_rows",
    )(residual, *pieces)


def body(
    sizes,
    block_input,
    cotangent,
    query_weight,
    key_weight,
    value_weight,
    output_weight,
    first_gain,
    first_shift,
    expert_in,
    expert_out,
    second_gain,
    second_shift,
    routes,
    route_gates,
    clip_threshold,
):
    dp, tensor = sizes["dp"], sizes["tensor"]
    inner = dp // OUTER
    tokens, features = block_input.shape
    columns = query_weight.shape[1]
    heads = columns // HD
    images = tokens // SEQ
    stride = up(SEQ, 8)
    padded = up(images * stride, 16)
    experts = expert_in.shape[0]
    mine = experts // 2
    half = mine // 2
    block = features // OUTER
    limit = 2 * CAP
    dp_at = lax.axis_index("dp")
    place = dp_at // inner
    tensor_at = lax.axis_index("tensor")
    low_bit = place >> 1 & 1

    def along(axis, size, flip):
        pairs = [(i, i ^ flip) for i in range(size)]
        return lambda value: lax.ppermute(value, axis, pairs)

    send_x = along("dp", dp, 1 * inner)
    send_low = along("dp", dp, 2 * inner)
    send_high = along("dp", dp, 4 * inner)
    send_core = along("tensor", tensor, 1)
    send_y = along("tensor", tensor, 2)

    def whole_block(value, axis):
        if inner == 1:
            return value
        every = lax.all_gather(value, "dp", axis=axis, tiled=True)
        return lax.dynamic_slice_in_dim(every, place * block, block, axis)

    def own_rows(value, axis):
        if inner == 1:
            return value
        shape = list(value.shape)
        shape[axis] = features
        every = lax.dynamic_update_slice_in_dim(jnp.zeros(shape, value.dtype), value, place * block, axis)
        return lax.psum_scatter(every, "dp", scatter_dimension=axis, tiled=True)

    packed = jnp.concatenate(
        (output_weight.T, query_weight, key_weight, value_weight), 1
    ).astype(BF16)
    packed = whole_block(packed, 0)
    norms = jnp.stack((first_gain, first_shift, second_gain, second_shift)).astype(BF16)
    norms = whole_block(norms, 1)
    norms = lax.dynamic_update_slice(jnp.zeros((EXTRA, features), BF16), norms, (0, place * block))
    own = jnp.concatenate((packed, norms), 0)[None]
    pair = jnp.concatenate((own, send_high(own)), 0)
    four = jnp.concatenate((pair, send_low(pair)), 0)
    four_x = send_x(four)
    four_y = send_y(four)
    two_a = send_x(four_y[:2])
    two_b = send_y(four_x[2:])

    def entries(t, x_bit, lows=(0, 1)):
        return tuple((t, block_flip(x_bit, low, high)) for low in lows for high in (0, 1))

    pieces = [four, four_x, four_y, two_a, two_b]
    layout = [entries(0, 0), entries(0, 1), entries(1, 0), entries(1, 1, (0,)), entries(1, 1, (1,))]
    for piece in (four, four_x, four_y, two_a, two_b):
        pieces.append(send_core(piece))
    layout += [tuple((t + 2, flip) for t, flip in group) for group in layout[:5]]
    gains = jnp.sum(jnp.concatenate((four[:, block:], four_x[:, block:]), 0).astype(F32), 0)

    w_in = whole_block(expert_in.astype(BF16), 1)
    w_out = whole_block(expert_out.astype(BF16), 2).swapaxes(1, 2)
    both = jnp.stack((w_in, w_out), 1)
    both, _ = lax.optimization_barrier((both, four))
    chunks = []
    for c in range(2):
        keep = lax.dynamic_slice_in_dim(both, low_bit * mine + c * half, half, 0)
        give = lax.dynamic_slice_in_dim(both, (1 - low_bit) * mine + c * half, half, 0)
        got_low = send_low(give)
        got = [keep, got_low, send_high(keep), send_high(got_low)]
        got += [send_x(w) for w in got]
        chunks.append(got)
    expert_layout = tuple(
        block_flip(x_bit, low, high) for x_bit in (0, 1) for high in (0, 1) for low in (0, 1)
    )

    table = jnp.concatenate((routes.T.astype(F32), route_gates.T), 0)
    picks = routes.shape[1]
    table = table.reshape(2 * picks, tensor, images, SEQ)
    table = jnp.pad(table, ((0, 0), (0, 0), (0, 0), (0, stride - SEQ)), constant_values=-1)
    table = table.reshape(2 * picks, tensor, images * stride)
    table = jnp.pad(table, ((0, 0), (0, 0), (0, padded - images * stride)), constant_values=-1)
    table = jnp.stack((table, send_low(table)))
    table = table.reshape(2, 2 * picks, 2, 2, padded)
    table = jnp.where(tensor_at >> 1 & 1 == 1, table[:, :, ::-1], table)
    table = jnp.where(tensor_at & 1 == 1, table[:, :, :, ::-1], table)
    table = table.transpose(1, 3, 0, 2, 4).reshape(2 * picks, 8, padded)
    ids = (low_bit * mine + jnp.arange(mine)).astype(F32)[None, :, None, None]
    hits = table[:picks, None] == ids
    chosen = jnp.any(hits, 0)
    gates = jnp.sum(jnp.where(hits, table[picks:, None], 0.0), 0)
    order = lax.broadcasted_iota(jnp.int32, (padded, padded), 0) < lax.broadcasted_iota(
        jnp.int32, (padded, padded), 1
    )
    before = jnp.dot(
        chosen.reshape(-1, padded).astype(BF16), order.astype(BF16), preferred_element_type=F32
    ).reshape(chosen.shape)
    counts = jnp.sum(chosen.astype(F32), -1)
    ahead = (jnp.arange(8)[:, None] < jnp.arange(8)[None, :]).astype(F32)
    starts = jnp.sum(counts[:, :, None] * ahead[None], 1)
    slots = jnp.where(chosen, starts[:, :, None] + before, -1.0).astype(jnp.int32)
    totals = jnp.sum(counts, 1)
    scalars = jnp.concatenate((starts.reshape(-1), counts.reshape(-1), totals)).astype(jnp.int32)
    slot_columns = slots.transpose(1, 2, 0)
    gate_columns = gates.transpose(1, 2, 0)

    def everyone(rows):
        by_low = send_low(rows)
        by_y = send_y(rows)
        near = [rows, by_y, by_low, send_y(by_low)]
        return near + [send_core(piece) for piece in near]

    def to_owner(send, keep):
        near = send_core(send)
        sums = [keep[i] + near[i] for i in range(4)]
        far = sums[2] + send_y(sums[3])
        return (sums[0], send_y(sums[1]), send_low(far))

    cot_half = spread(cotangent, images, stride, padded)
    cot_slots = dispatch(scalars, everyone(cot_half), slots, gates, limit)

    place_word = place.astype(jnp.int32).reshape(1)
    residual, second, first, weights, kept, peaks = attention_forward(
        place_word, block_input, gains, pieces, layout, images, stride, padded, tensor, heads
    )

    x_slots = dispatch(scalars, everyone(second), slots, None, limit)
    results, shares = [], []
    for c in range(2):
        info = jnp.concatenate((place_word, totals[c * half : (c + 1) * half].astype(jnp.int32)))
        y, dx, keep, send = expert_math(
            info, x_slots, cot_slots, chunks[c], expert_layout, c * half, limit
        )
        results.append((y, dx))
        rows = keep.shape[2] // 2
        other = send_x(send)
        far = send_high(keep[:, :, rows:] + other[:, :, rows:])
        near = (keep[:, :, :rows] + other[:, :, :rows]).astype(F32) + far.astype(F32)
        shares.append((near[:, :, :block], send_low(near[:, :, block:].astype(BF16))))
    grad_pieces = to_owner(*combine(scalars, [dx for _, dx in results], slot_columns, None))
    mixture_pieces = to_owner(*combine(scalars, [y for y, _ in results], slot_columns, gate_columns))

    peak = peaks[:, 0, :heads].reshape(2, 2, heads)
    peak = jnp.where(tensor_at & 1 == 1, peak[::-1], peak)
    peak = jnp.where(tensor_at >> 1 & 1 == 1, peak[:, ::-1], peak)
    peak = peak.transpose(1, 0, 2).reshape(tensor * heads)
    extra = jnp.zeros((EXTRA, features), F32)
    if inner == 1:
        device = dp_at * tensor + tensor_at
        high = lax.reduce_precision(peak, 8, 7)
        rest = lax.reduce_precision(peak - high, 8, 7)
        is_mine = (jnp.arange(dp * tensor) == device)[None, :, None]
        words = jnp.where(is_mine, jnp.stack((high, rest))[:, None, :], 0.0).reshape(2, -1)
        extra = extra.at[4:6, : words.shape[1]].set(words)
    input_grad, keep, send = attention_backward(
        block_input, cotangent, residual, grad_pieces, first, weights, kept, gains, extra, images, stride, heads
    )
    block_output = finish(residual, mixture_pieces, tokens, images, stride)

    own_share = jnp.concatenate([near for near, _ in shares], 0).astype(BF16)
    far_share = jnp.concatenate([far for _, far in shares], 0)
    grads = jnp.concatenate(
        (
            jnp.where(low_bit == 0, own_share, far_share),
            jnp.where(low_bit == 0, far_share, own_share),
        ),
        0,
    ).astype(F32)
    expert_in_grad = own_rows(grads[:, 0], 1)
    expert_out_grad = own_rows(grads[:, 1].swapaxes(1, 2), 2)

    near = send_core(send)
    upper = send_y(keep[1] + near[1])
    total = keep[0] + near[0] + upper
    if inner == 1:
        total = lax.all_to_all(total, "dp", 0, 0, tiled=True)
        total = jnp.sum(total.astype(F32), 0)
        words = total[block:]
        total = total[:block]
        peak = jnp.sum(words[4:6, : dp * tensor * tensor * heads], 0).reshape(dp * tensor, tensor * heads)
        peak = jnp.max(peak, 0)
    else:
        words = lax.psum(total[0, block:].astype(F32), "dp")
        total = total[:, :block].reshape(features, features).astype(F32)
        total = lax.psum_scatter(total, "dp", scatter_dimension=0, tiled=True)
        peak = lax.pmax(peak, ("dp", "tensor"))
    head_maxima = lax.dynamic_slice_in_dim(peak, tensor_at * heads, heads, 0)
    vectors = lax.dynamic_slice_in_dim(words[:4], dp_at * (features // dp), features // dp, 1)
    output_grad, query_grad, key_grad, value_grad = (
        total[:, i * columns : (i + 1) * columns] for i in range(4)
    )
    factor = jnp.minimum(1.0, clip_threshold / jnp.maximum(head_maxima, 1.0))
    column_scale = jnp.repeat(jnp.sqrt(factor), HD)
    return (
        block_output,
        input_grad,
        query_grad,
        key_grad,
        value_grad,
        output_grad.T,
        vectors[0],
        vectors[1],
        expert_in_grad,
        expert_out_grad,
        vectors[2],
        vectors[3],
        query_weight * column_scale[None, :],
        key_weight * column_scale[None, :],
        head_maxima,
    )


def solution(mesh):
    rows = P(("dp", "tensor"), None)
    by_column, by_row, by_dp = P("dp", "tensor"), P("tensor", "dp"), P("dp")
    up_spec, down_spec = P(None, "dp", "tensor"), P(None, "tensor", "dp")
    sizes = dict(mesh.shape)
    return jax.shard_map(
        functools.partial(body, sizes),
        mesh=mesh,
        in_specs=(
            rows, rows, by_column, by_column, by_column, by_row, by_dp, by_dp, up_spec, down_spec,
            by_dp, by_dp, P("dp", None), P("dp", None), P("tensor"),
        ),
        out_specs=(
            rows, rows, by_column, by_column, by_column, by_row, by_dp, by_dp, up_spec, down_spec,
            by_dp, by_dp, by_column, by_column, P("tensor"),
        ),
        check_vma=False,
    )
```

time: 1860 us -> 686 us (0.37)
  waiting for transfers between devices: 820 us -> 326 us
  blocking collectives: 347 us -> 0 us
  local copies, waits for them, and re-layouts: 281 us -> 29.9 us
  Pallas kernels: 0 us -> 205 us
  matrix products: 201 us -> 0.83 us
  other arithmetic: 174 us -> 40.6 us
  starting transfers between devices: 8.42 us -> 71.2 us
    reduce_scatter x2 -> x0, waiting for transfers between devices: 634 us -> none  [the longest x1 317 us: body(): lax.psum_scatter(grad_up, 'dp', scatter_dimension=1, tiled=True)]
    ppermute x0 -> x56, waiting for transfers between devices: none -> 326 us  [along(): return lambda value: lax.ppermute(value, axis, pairs)]
    pallas_call x0 -> x10, Pallas kernels: none -> 205 us  [the longest x2 58.6 us: expert_math(): pl.pallas_call(functools.partial(expert_kernel, layout), grid=(experts,),...]
    dot_general x17 -> x1, matrix products: 198 us -> 0.83 us  [body(): jnp.dot(chosen.reshape(-1, padded).astype(BF16), order.astype(BF16), pref...]
    unnamed x5 -> x0, blocking collectives: 193 us -> none
    all_gather x6 -> x0, waiting for transfers between devices: 177 us -> none  [the longest x1 117 us: expert_params(): lax.all_gather(to_half(expert_out), 'dp', axis=2, tiled=True)]
    all_gather x4 -> x0, blocking collectives: 126 us -> none  [the longest x1 33 us: body(): lax.all_gather(to_half(output_weight), 'dp', axis=1, tiled=True)]
    gather x4 -> x0, local copies, waits for them, and re-layouts: 103 us -> none  [the longest x1 26.8 us: body(): jnp.take(cotangent_rows, slot_token, axis=0).astype(jnp.float32)]
  transfers between devices with their start and end apart: 16 -> 57, of which waited for: 7 -> 24; matrix products, arithmetic and copies ran while one was open for 24% -> 8% of each run, Pallas kernels for 0% -> 23%
where the time goes in v1:
time: 686 us; the launch traced here: 676 us
  waiting for transfers between devices  326 us (48%)
  Pallas kernels  205 us (30%)
  starting transfers between devices  71.2 us (10%)
  other arithmetic  40.6 us (6%)
  local copies, waits for them, and re-layouts  29.9 us (4%)
    ppermute x56, waiting for transfers between devices, along(): return lambda value: lax.ppermute(value, axis, pairs)  326 us
    ppermute x56, starting transfers between devices, along(): return lambda value: lax.ppermute(value, axis, pairs)  66.5 us
    pallas_call x2, Pallas kernels, expert_math(): pl.pallas_call(functools.partial(expert_kernel, layout), grid=(experts,),...  58.6 us
    pallas_call x2, Pallas kernels, dispatch(): pl.pallas_call(functools.partial(dispatch_kernel, gated), grid=(experts,)...  41.7 us
    pallas_call x1, Pallas kernels, attention_backward(): pl.pallas_call(functools.partial(attention_backward_kernel, images, strid...  41.3 us
    pallas_call x2, Pallas kernels, combine(): pl.pallas_call(functools.partial(combine_kernel, gated, len(sources)), gr...  38.6 us
    pallas_call x1, Pallas kernels, attention_forward(): pl.pallas_call(functools.partial(attention_forward_kernel, images, stride...  22.4 us
  transfers between devices with their start and end apart: 57, of which 24 were waited for; matrix products, arithmetic and copies ran while one was open for 8% of the time, Pallas kernels for 23%

profile of v1, /device:TPU:0, one launch (start us, length us, event | category | flops | bytes accessed | tf_op | source)
XLA Modules:
  0.0 675.5 jit_solution(656050443471328098)
XLA Ops:
  11.0 7.3 %collective-permute-done = bf16[1,112,768]{2,1,0:T(8,128)(2,1)S(1)} collective-permute-done((bf16[1,112,768]{2,1,0:T(8,128)(2,1)S(1)}, bf16[1,112,768]{2,1,0:T(8,128)(2,1)S(1)}, u32[]{:S(2)}, u32[]{:S(2)}) %collective-permute-start) | collective-permute-done | bytes 172064 | tf_op jit(solution)/shard_map/ppermute | solution.py:561
  23.6 4.6 collective-permute-done.1
  34.4 10.2 %collective-permute-done.2.refs_4_ = bf16[4,112,768]{2,1,0:T(8,128)(2,1)} collective-permute-done((bf16[4,112,768]{2,1,0:T(8,128)(2,1)}, bf16[4,112,768]{2,1,0:T(8,128)(2,1)}, u32[]{:S(2)}, u32[]{:S(2)}) %collective-permute-start.2) | collective-permute-done | bytes 688160 | tf_op jit(solution)/shard_map/ppermute | solution.py:561
  65.6 22.4 %attention_forward.1 = (f32[608,768]{1,0:T(8,128)}, bf16[608,768]{1,0:T(8,128)(2,1)}, bf16[608,768]{1,0:T(8,128)(2,1)}, bf16[4,768,768]{2,1,0:T(8,128)(2,1)}, bf...) custom-call(s32[1]{0:T(128)} %bitcast.refs_0_, f32[591,768]{1,0:T(8,128)} %refs_0_.1, ...), custom_call_target="tpu_custom_call" | custom-call | flops 14918300672 | bytes 20000000 | tf_op jit(solution)/shard_map/attention_forward/pallas_call | solution.py:141
  96.9 14.7 %collective-permute-done.33.refs_4_ = bf16[2,2,96,768]{3,2,1,0:T(8,128)(2,1)S(1)} collective-permute-done((bf16[2,2,96,768]{3,2,1,0:T(8,128)(2,1)S(1)}, bf16[2,2,96,768]{3,2,1,0:T(8,128)(2,1)S(1)}, u32[]{:S(2)}, u32[]{:S(2)}) %collective-permute-start.33) | collective-permute-done | bytes 589856 | tf_op jit(solution)/shard_map/ppermute | solution.py:561
  117.1 14.1 %collective-permute-done.34.refs_5_ = bf16[2,2,96,768]{3,2,1,0:T(8,128)(2,1)} collective-permute-done((bf16[2,2,96,768]{3,2,1,0:T(8,128)(2,1)}, bf16[2,2,96,768]{3,2,1,0:T(8,128)(2,1)}, u32[]{:S(2)}, u32[]{:S(2)}) %collective-permute-start.34) | collective-permute-done | bytes 589856 | tf_op jit(solution)/shard_map/ppermute | solution.py:561
  131.7 12.4 %collective-permute-done.26.refs_4_ = bf16[2,2,96,768]{3,2,1,0:T(8,128)(2,1)S(1)} collective-permute-done((bf16[2,2,96,768]{3,2,1,0:T(8,128)(2,1)}, bf16[2,2,96,768]{3,2,1,0:T(8,128)(2,1)S(1)}, u32[]{:S(2)}, u32[]{:S(2)}) %collective-permute-start.26) | collective-permute-done | bytes 589856 | tf_op jit(solution)/shard_map/ppermute | solution.py:561
  150.7 17.2 %collective-permute-done.12.refs_2_ = bf16[608,768]{1,0:T(8,128)(2,1)S(1)} collective-permute-done((bf16[608,768]{1,0:T(8,128)(2,1)}, bf16[608,768]{1,0:T(8,128)(2,1)S(1)}, u32[]{:S(2)}, u32[]{:S(2)}) %collective-permute-start.12) | collective-permute-done | bytes 933920 | tf_op jit(solution)/shard_map/ppermute | solution.py:561
  167.9 19.0 %collective-permute-done.14.refs_4_ = bf16[608,768]{1,0:T(8,128)(2,1)S(1)} collective-permute-done((bf16[608,768]{1,0:T(8,128)(2,1)}, bf16[608,768]{1,0:T(8,128)(2,1)S(1)}, u32[]{:S(2)}, u32[]{:S(2)}) %collective-permute-start.14) | collective-permute-done | bytes 933920 | tf_op jit(solution)/shard_map/ppermute | solution.py:561
  190.9 21.4 %dispatch_gated.1.refs_2_ = bf16[4,2384,768]{2,1,0:T(8,128)(2,1)} custom-call(s32[68]{0:T(128)S(1)} %maximum_convert_fusion.1.refs_0_, bf16[608,768]{1,0:T(8,128)(2,1)S(1)} %spread_rows.1.refs_1_, bf16[608,768]{1,0:T(8,128)(2,1)} %collective-permute-done.19.refs_2_, bf16[608,768]{1,0:T(8,128)(2,1)} %collective-permute-done.20.refs_3_, ...), custom_call_target="tpu_custom_call" | custom-call | flops 7650410496 | bytes 20000000 | tf_op jit(solution)/shard_map/dispatch_gated/pallas_call | solution.py:328
  212.3 5.3 collective-permute-done.35.refs_6_
  224.3 20.3 %dispatch.1.refs_1_ = bf16[4,2384,768]{2,1,0:T(8,128)(2,1)} custom-call(s32[68]{0:T(128)S(1)} %maximum_convert_fusion.1.refs_0_, bf16[608,768]{1,0:T(8,128)(2,1)} %get-tuple-element.50.refs_1_, bf16[608,768]{1,0:T(8,128)(2,1)S(1)} %collective-permute-done.12.refs_2_, bf16[608,768]{1,0:T(8,128)(2,1)} %collective-permute-done.13.refs_3_, ...), custom_call_target="tpu_custom_call" | custom-call | flops 7650410496 | bytes 20000000 | tf_op jit(solution)/shard_map/dispatch/pallas_call | solution.py:328
  244.6 15.2 %collective-permute-done.27.refs_5_ = bf16[2,2,96,768]{3,2,1,0:T(8,128)(2,1)} collective-permute-done((bf16[2,2,96,768]{3,2,1,0:T(8,128)(2,1)}, bf16[2,2,96,768]{3,2,1,0:T(8,128)(2,1)}, u32[]{:S(2)}, u32[]{:S(2)}) %collective-permute-start.27) | collective-permute-done | bytes 589856 | tf_op jit(solution)/shard_map/ppermute | solution.py:561
  264.3 7.6 %collective-permute-done.28.refs_6_ = bf16[2,2,96,768]{3,2,1,0:T(8,128)(2,1)} collective-permute-done((bf16[2,2,96,768]{3,2,1,0:T(8,128)(2,1)}, bf16[2,2,96,768]{3,2,1,0:T(8,128)(2,1)}, u32[]{:S(2)}, u32[]{:S(2)}) %collective-permute-start.28) | collective-permute-done | bytes 589856 | tf_op jit(solution)/shard_map/ppermute | solution.py:561
  273.6 29.1 %expert_math.3 = (bf16[2,2384,768]{2,1,0:T(8,128)(2,1)}, bf16[2,2384,768]{2,1,0:T(8,128)(2,1)}, bf16[2,2,384,768]{3,2,1,0:T(8,128)(2,1)}, bf16[2,2,384,768]{3,2,1,0:T(8,128)(2,1)}) custom-call(s32[3]{0:T(128)} %pad_add_fusion.1.refs_0_, bf16[4,2384,768]{2,1,0:T(8,128)(2,1)} %dispatch.1.refs_1_, bf16[4,2384,768]{2,1,0:T(8,128)(2,1)} %dispatch_gated.1.refs_2_, ...), custom_call_target="tpu_custom_call" | custom-call | flops 22422749184 | bytes 30000000 | tf_op jit(solution)/shard_map/expert_math/pallas_call | solution.py:394
  302.8 9.6 %collective-permute-done.32.refs_10_ = bf16[2,2,96,768]{3,2,1,0:T(8,128)(2,1)} collective-permute-done((bf16[2,2,96,768]{3,2,1,0:T(8,128)(2,1)}, bf16[2,2,96,768]{3,2,1,0:T(8,128)(2,1)}, u32[]{:S(2)}, u32[]{:S(2)}) %collective-permute-start.32) | collective-permute-done | bytes 589856 | tf_op jit(solution)/shard_map/ppermute | solution.py:561
  312.4 29.5 %expert_math.2 = (bf16[2,2384,768]{2,1,0:T(8,128)(2,1)}, bf16[2,2384,768]{2,1,0:T(8,128)(2,1)}, bf16[2,2,384,768]{3,2,1,0:T(8,128)(2,1)}, bf16[2,2,384,768]{3,2,1,0:T(8,128)(2,1)}) custom-call(s32[3]{0:T(128)} %pad_add_fusion.refs_0_, bf16[4,2384,768]{2,1,0:T(8,128)(2,1)} %dispatch.1.refs_1_, bf16[4,2384,768]{2,1,0:T(8,128)(2,1)} %dispatch_gated.1.refs_2_, ...), custom_call_target="tpu_custom_call" | custom-call | flops 22422749184 | bytes 30000000 | tf_op jit(solution)/shard_map/expert_math/pallas_call | solution.py:394
  341.9 18.5 %combine.1 = (bf16[4,608,768]{2,1,0:T(8,128)(2,1)}, bf16[4,608,768]{2,1,0:T(8,128)(2,1)}) custom-call(s32[68]{0:T(128)S(1)} %maximum_convert_fusion.1.refs_0_, bf16[2,2384,768]{2,1,0:T(8,128)(2,1)} %get-tuple-element.56.refs_1_, bf16[2,2384,768]{2,1,0:T(8,128)(2,1)} %get-tuple-element.57.refs_2_, s32[8,608,4]{2,1,0:T(8,128)S(1)} %fusion.1.refs_3_), custom_call_target="tpu_custom_call" | custom-call | flops 7650410496 | bytes 20000000 | tf_op jit(solution)/shard_map/combine/pallas_call | solution.py:470
  360.4 6.7 collective-permute-done.44
  367.1 4.6 fusion.8
  374.6 20.7 %collective-permute-done.46 = bf16[608,768]{1,0:T(8,128)(2,1)} collective-permute-done((bf16[608,768]{1,0:T(8,128)(2,1)S(1)}, bf16[608,768]{1,0:T(8,128)(2,1)}, u32[]{:S(2)}, u32[]{:S(2)}) %collective-permute-start.46) | collective-permute-done | bytes 933920 | tf_op jit(solution)/shard_map/ppermute | solution.py:561
  397.2 6.7 collective-permute-start.47
  406.6 8.0 %collective-permute-done.45.refs_4_ = bf16[608,768]{1,0:T(8,128)(2,1)} collective-permute-done((bf16[608,768]{1,0:T(8,128)(2,1)}, bf16[608,768]{1,0:T(8,128)(2,1)}, u32[]{:S(2)}, u32[]{:S(2)}) %collective-permute-start.45) | collective-permute-done | bytes 933920 | tf_op jit(solution)/shard_map/ppermute | solution.py:561
  414.5 8.9 %collective-permute-done.47.refs_5_ = bf16[608,768]{1,0:T(8,128)(2,1)} collective-permute-done((bf16[608,768]{1,0:T(8,128)(2,1)S(1)}, bf16[608,768]{1,0:T(8,128)(2,1)}, u32[]{:S(2)}, u32[]{:S(2)}) %collective-permute-start.47) | collective-permute-done | bytes 933920 | tf_op jit(solution)/shard_map/ppermute | solution.py:561
  423.4 41.3 %attention_backward.1 = (f32[591,768]{1,0:T(8,128)}, bf16[2,8,112,768]{3,2,1,0:T(8,128)(2,1)}, bf16[2,8,112,768]{3,2,1,0:T(8,128)(2,1)}) custom-call(f32[591,768]{1,0:T(8,128)} %refs_0_.1, f32[591,768]{1,0:T(8,128)} %refs_1_.3, f32[608,768]{1,0:T(8,128)} %get-tuple-element.49.res_ref.refs_2_, bf16[608,768]{1,0:T(8,128)(2,1)} %get-tuple-element.137.refs_3_, ...), custom_call_target="tpu_custom_call" | custom-call | flops 11475615744 | bytes 30000000 | tf_op jit(solution)/shard_map/attention_backward/pallas_call | solution.py:261
  470.4 20.1 %combine_gated.1 = (bf16[4,608,768]{2,1,0:T(8,128)(2,1)}, bf16[4,608,768]{2,1,0:T(8,128)(2,1)}) custom-call(s32[68]{0:T(128)S(1)} %maximum_convert_fusion.1.refs_0_, bf16[2,2384,768]{2,1,0:T(8,128)(2,1)} %get-tuple-element.52.refs_1_, bf16[2,2384,768]{2,1,0:T(8,128)(2,1)} %get-tuple-element.53.refs_2_, s32[8,608,4]{2,1,0:T(8,128)S(1)} %fusion.1.refs_3_, ...), custom_call_target="tpu_custom_call" | custom-call | flops 7650410496 | bytes 20000000 | tf_op jit(solution)/shard_map/combine_gated/pallas_call | solution.py:470
  494.9 23.8 %collective-permute-done.52 = bf16[2,2,384,768]{3,2,1,0:T(8,128)(2,1)} collective-permute-done((bf16[2,2,384,768]{3,2,1,0:T(8,128)(2,1)}, bf16[2,2,384,768]{3,2,1,0:T(8,128)(2,1)}, u32[]{:S(2)}, u32[]{:S(2)}) %collective-permute-start.52) | collective-permute-done | bytes 2359328 | tf_op jit(solution)/shard_map/ppermute | solution.py:561
  524.7 47.9 %collective-permute-done.51 = bf16[2,2,192,768]{3,2,1,0:T(8,128)(2,1)S(1)} collective-permute-done((bf16[2,2,192,768]{3,2,1,0:T(8,128)(2,1)S(1)}, bf16[2,2,192,768]{3,2,1,0:T(8,128)(2,1)S(1)}, u32[]{:S(2)}, u32[]{:S(2)}) %collective-permute-start.51) | collective-permute-done | bytes 1179680 | tf_op jit(solution)/shard_map/ppermute | solution.py:561
  575.5 21.9 %collective-permute-done.53 = bf16[2,2,192,768]{3,2,1,0:T(8,128)(2,1)S(1)} collective-permute-done((bf16[2,2,192,768]{3,2,1,0:T(8,128)(2,1)S(1)}, bf16[2,2,192,768]{3,2,1,0:T(8,128)(2,1)S(1)}, u32[]{:S(2)}, u32[]{:S(2)}) %collective-permute-start.53) | collective-permute-done | bytes 1179680 | tf_op jit(solution)/shard_map/ppermute | solution.py:561
  601.9 4.7 all-to-all-start
  617.1 27.7 %collective-permute-done.55 = bf16[2,2,96,768]{3,2,1,0:T(8,128)(2,1)S(1)} collective-permute-done((bf16[2,2,96,768]{3,2,1,0:T(8,128)(2,1)}, bf16[2,2,96,768]{3,2,1,0:T(8,128)(2,1)S(1)}, u32[]{:S(2)}, u32[]{:S(2)}) %collective-permute-start.55) | collective-permute-done | bytes 589856 | tf_op jit(solution)/shard_map/ppermute | solution.py:561
  653.3 15.8 %collective-permute-done.43.c_ref = bf16[608,768]{1,0:T(8,128)(2,1)S(1)} collective-permute-done((bf16[608,768]{1,0:T(8,128)(2,1)S(1)}, bf16[608,768]{1,0:T(8,128)(2,1)S(1)}, u32[]{:S(2)}, u32[]{:S(2)}) %collective-permute-start.43) | collective-permute-done | bytes 933920 | tf_op jit(solution)/shard_map/ppermute | solution.py:561
  (252 shorter events, 136.7 us)
Async XLA Ops:
  65.3 46.3 %collective-permute-start.33 = (bf16[2,2,96,768]{3,2,1,0:T(8,128)(2,1)S(1)}, bf16[2,2,96,768]{3,2,1,0:T(8,128)(2,1)S(1)}, u32[]{:S(2)}, u32[]{:S(2)}) collective-permute-start(bf16[2,2,96,768]{3,2,1,0:T(8,128)(2,1)S(1)} %get-tuple-element.145), channel_id=1, source_target_pairs={{0,8},{4,12},{8,0},{12,4},{16,24},{20,28},{24,16},{28,20},{1,9},{5... | collective-permute-start | bytes 1769480 | tf_op jit(solution)/shard_map/ppermute | solution.py:561
  88.1 56.6 %collective-permute-start.13 = (bf16[608,768]{1,0:T(8,128)(2,1)}, bf16[608,768]{1,0:T(8,128)(2,1)}, u32[]{:S(2)}, u32[]{:S(2)}) collective-permute-start(bf16[608,768]{1,0:T(8,128)(2,1)} %get-tuple-element.50.refs_1_), channel_id=1, source_target_pairs={{0,8},{4,12},{8,0},{12,4},{16,24},{20,28},{24,16},{28,20},{1,9},{5... | collective-permute-start | bytes 2801672 | tf_op jit(solution)/shard_map/ppermute | solution.py:561
  89.9 41.3 %collective-permute-start.34 = (bf16[2,2,96,768]{3,2,1,0:T(8,128)(2,1)}, bf16[2,2,96,768]{3,2,1,0:T(8,128)(2,1)}, u32[]{:S(2)}, u32[]{:S(2)}) collective-permute-start(bf16[2,2,96,768]{3,2,1,0:T(8,128)(2,1)} %get-tuple-element.146.refs_3_), channel_id=1, source_target_pairs={{0,16},{4,20},{8,24},{12,28},{16,0},{20,4},{24,8},{28,12},{1,17},{... | collective-permute-start | bytes 1769480 | tf_op jit(solution)/shard_map/ppermute | solution.py:561
  93.4 37.8 %collective-permute-start.36 = (bf16[2,2,96,768]{3,2,1,0:T(8,128)(2,1)}, bf16[2,2,96,768]{3,2,1,0:T(8,128)(2,1)}, u32[]{:S(2)}, u32[]{:S(2)}) collective-permute-start(bf16[2,2,96,768]{3,2,1,0:T(8,128)(2,1)} %get-tuple-element.146.refs_3_), channel_id=1, source_target_pairs={{0,4},{4,0},{8,12},{12,8},{16,20},{20,16},{24,28},{28,24},{1,5},{5... | collective-permute-start | bytes 1769480 | tf_op jit(solution)/shard_map/ppermute | solution.py:561
  96.0 48.1 %collective-permute-start.26 = (bf16[2,2,96,768]{3,2,1,0:T(8,128)(2,1)}, bf16[2,2,96,768]{3,2,1,0:T(8,128)(2,1)S(1)}, u32[]{:S(2)}, u32[]{:S(2)}) collective-permute-start(bf16[2,2,96,768]{3,2,1,0:T(8,128)(2,1)} %get-tuple-element.147), channel_id=1, source_target_pairs={{0,8},{4,12},{8,0},{12,4},{16,24},{20,28},{24,16},{28,20},{1,9},{5... | collective-permute-start | bytes 1769480 | tf_op jit(solution)/shard_map/ppermute | solution.py:561
  111.6 35.2 %collective-permute-start.21 = (bf16[608,768]{1,0:T(8,128)(2,1)}, bf16[608,768]{1,0:T(8,128)(2,1)}, u32[]{:S(2)}, u32[]{:S(2)}) collective-permute-start(bf16[608,768]{1,0:T(8,128)(2,1)} %collective-permute-done.20.refs_3_), channel_id=1, source_target_pairs={{0,2},{1,3},{2,0},{3,1},{4,6},{5,7},{6,4},{7,5},{8,10},{9,11},{10,... | collective-permute-start | bytes 2801672 | tf_op jit(solution)/shard_map/ppermute | solution.py:561
  144.6 42.2 %collective-permute-start.14 = (bf16[608,768]{1,0:T(8,128)(2,1)}, bf16[608,768]{1,0:T(8,128)(2,1)S(1)}, u32[]{:S(2)}, u32[]{:S(2)}) collective-permute-start(bf16[608,768]{1,0:T(8,128)(2,1)} %collective-permute-done.13.refs_3_), channel_id=1, source_target_pairs={{0,2},{1,3},{2,0},{3,1},{4,6},{5,7},{6,4},{7,5},{8,10},{9,11},{10,... | collective-permute-start | bytes 2801672 | tf_op jit(solution)/shard_map/ppermute | solution.py:561
  146.8 40.2 %collective-permute-start.25 = (bf16[608,768]{1,0:T(8,128)(2,1)}, bf16[608,768]{1,0:T(8,128)(2,1)S(1)}, u32[]{:S(2)}, u32[]{:S(2)}) collective-permute-start(bf16[608,768]{1,0:T(8,128)(2,1)} %collective-permute-done.21.refs_4_), channel_id=1, source_target_pairs={{0,1},{1,0},{2,3},{3,2},{4,5},{5,4},{6,7},{7,6},{8,9},{9,8},{10,11... | collective-permute-start | bytes 2801672 | tf_op jit(solution)/shard_map/ppermute | solution.py:561
  150.1 67.6 %collective-permute-start.15 = (bf16[608,768]{1,0:T(8,128)(2,1)}, bf16[608,768]{1,0:T(8,128)(2,1)S(1)}, u32[]{:S(2)}, u32[]{:S(2)}) collective-permute-start(bf16[608,768]{1,0:T(8,128)(2,1)} %get-tuple-element.50.refs_1_), channel_id=1, source_target_pairs={{0,1},{1,0},{2,3},{3,2},{4,5},{5,4},{6,7},{7,6},{8,9},{9,8},{10,11... | collective-permute-start | bytes 2801672 | tf_op jit(solution)/shard_map/ppermute | solution.py:561
  150.6 69.1 %collective-permute-start.17 = (bf16[608,768]{1,0:T(8,128)(2,1)}, bf16[608,768]{1,0:T(8,128)(2,1)S(1)}, u32[]{:S(2)}, u32[]{:S(2)}) collective-permute-start(bf16[608,768]{1,0:T(8,128)(2,1)} %collective-permute-done.13.refs_3_), channel_id=1, source_target_pairs={{0,1},{1,0},{2,3},{3,2},{4,5},{5,4},{6,7},{7,6},{8,9},{9,8},{10,11... | collective-permute-start | bytes 2801672 | tf_op jit(solution)/shard_map/ppermute | solution.py:561
  167.9 51.5 %collective-permute-start.16 = (bf16[608,768]{1,0:T(8,128)(2,1)S(1)}, bf16[608,768]{1,0:T(8,128)(2,1)S(1)}, u32[]{:S(2)}, u32[]{:S(2)}) collective-permute-start(bf16[608,768]{1,0:T(8,128)(2,1)S(1)} %collective-permute-done.12.refs_2_), channel_id=1, source_target_pairs={{0,1},{1,0},{2,3},{3,2},{4,5},{5,4},{6,7},{7,6},{8,9},{9,8},{10,11... | collective-permute-start | bytes 2801672 | tf_op jit(solution)/shard_map/ppermute | solution.py:561
  186.9 35.7 %collective-permute-start.18 = (bf16[608,768]{1,0:T(8,128)(2,1)S(1)}, bf16[608,768]{1,0:T(8,128)(2,1)S(1)}, u32[]{:S(2)}, u32[]{:S(2)}) collective-permute-start(bf16[608,768]{1,0:T(8,128)(2,1)S(1)} %collective-permute-done.14.refs_4_), channel_id=1, source_target_pairs={{0,1},{1,0},{2,3},{3,2},{4,5},{5,4},{6,7},{7,6},{8,9},{9,8},{10,11... | collective-permute-start | bytes 2801672 | tf_op jit(solution)/shard_map/ppermute | solution.py:561
  217.6 42.1 %collective-permute-start.27 = (bf16[2,2,96,768]{3,2,1,0:T(8,128)(2,1)}, bf16[2,2,96,768]{3,2,1,0:T(8,128)(2,1)}, u32[]{:S(2)}, u32[]{:S(2)}) collective-permute-start(bf16[2,2,96,768]{3,2,1,0:T(8,128)(2,1)} %get-tuple-element.148.refs_3_), channel_id=1, source_target_pairs={{0,16},{4,20},{8,24},{12,28},{16,0},{20,4},{24,8},{28,12},{1,17},{... | collective-permute-start | bytes 1769480 | tf_op jit(solution)/shard_map/ppermute | solution.py:561
  217.6 44.2 %collective-permute-start.37 = (bf16[2,2,96,768]{3,2,1,0:T(8,128)(2,1)S(1)}, bf16[2,2,96,768]{3,2,1,0:T(8,128)(2,1)S(1)}, u32[]{:S(2)}, u32[]{:S(2)}) collective-permute-start(bf16[2,2,96,768]{3,2,1,0:T(8,128)(2,1)S(1)} %copy-done.25), channel_id=1, source_target_pairs={{0,4},{4,0},{8,12},{12,8},{16,20},{20,16},{24,28},{28,24},{1,5},{5... | collective-permute-start | bytes 1769480 | tf_op jit(solution)/shard_map/ppermute | solution.py:561
  219.4 42.0 %collective-permute-start.38 = (bf16[2,2,96,768]{3,2,1,0:T(8,128)(2,1)}, bf16[2,2,96,768]{3,2,1,0:T(8,128)(2,1)S(1)}, u32[]{:S(2)}, u32[]{:S(2)}) collective-permute-start(bf16[2,2,96,768]{3,2,1,0:T(8,128)(2,1)} %collective-permute-done.34.refs_5_), channel_id=1, source_target_pairs={{0,4},{4,0},{8,12},{12,8},{16,20},{20,16},{24,28},{28,24},{1,5},{5... | collective-permute-start | bytes 1769480 | tf_op jit(solution)/shard_map/ppermute | solution.py:561
  219.7 52.2 %collective-permute-start.28 = (bf16[2,2,96,768]{3,2,1,0:T(8,128)(2,1)}, bf16[2,2,96,768]{3,2,1,0:T(8,128)(2,1)}, u32[]{:S(2)}, u32[]{:S(2)}) collective-permute-start(bf16[2,2,96,768]{3,2,1,0:T(8,128)(2,1)} %copy-done.26), channel_id=1, source_target_pairs={{0,16},{4,20},{8,24},{12,28},{16,0},{20,4},{24,8},{28,12},{1,17},{... | collective-permute-start | bytes 1769480 | tf_op jit(solution)/shard_map/ppermute | solution.py:561
  222.6 51.0 %collective-permute-start.39 = (bf16[2,2,96,768]{3,2,1,0:T(8,128)(2,1)}, bf16[2,2,96,768]{3,2,1,0:T(8,128)(2,1)}, u32[]{:S(2)}, u32[]{:S(2)}) collective-permute-start(bf16[2,2,96,768]{3,2,1,0:T(8,128)(2,1)} %collective-permute-done.35.refs_6_), channel_id=1, source_target_pairs={{0,4},{4,0},{8,12},{12,8},{16,20},{20,16},{24,28},{28,24},{1,5},{5... | collective-permute-start | bytes 1769480 | tf_op jit(solution)/shard_map/ppermute | solution.py:561
  259.7 43.0 %collective-permute-start.29 = (bf16[2,2,96,768]{3,2,1,0:T(8,128)(2,1)}, bf16[2,2,96,768]{3,2,1,0:T(8,128)(2,1)}, u32[]{:S(2)}, u32[]{:S(2)}) collective-permute-start(bf16[2,2,96,768]{3,2,1,0:T(8,128)(2,1)} %get-tuple-element.148.refs_3_), channel_id=1, source_target_pairs={{0,4},{4,0},{8,12},{12,8},{16,20},{20,16},{24,28},{28,24},{1,5},{5... | collective-permute-start | bytes 1769480 | tf_op jit(solution)/shard_map/ppermute | solution.py:561
  261.4 41.4 %collective-permute-start.30 = (bf16[2,2,96,768]{3,2,1,0:T(8,128)(2,1)S(1)}, bf16[2,2,96,768]{3,2,1,0:T(8,128)(2,1)}, u32[]{:S(2)}, u32[]{:S(2)}) collective-permute-start(bf16[2,2,96,768]{3,2,1,0:T(8,128)(2,1)S(1)} %copy-done.27), channel_id=1, source_target_pairs={{0,4},{4,0},{8,12},{12,8},{16,20},{20,16},{24,28},{28,24},{1,5},{5... | collective-permute-start | bytes 1769480 | tf_op jit(solution)/shard_map/ppermute | solution.py:561
  262.6 40.1 %collective-permute-start.31 = (bf16[2,2,96,768]{3,2,1,0:T(8,128)(2,1)}, bf16[2,2,96,768]{3,2,1,0:T(8,128)(2,1)}, u32[]{:S(2)}, u32[]{:S(2)}) collective-permute-start(bf16[2,2,96,768]{3,2,1,0:T(8,128)(2,1)} %collective-permute-done.27.refs_5_), channel_id=1, source_target_pairs={{0,4},{4,0},{8,12},{12,8},{16,20},{20,16},{24,28},{28,24},{1,5},{5... | collective-permute-start | bytes 1769480 | tf_op jit(solution)/shard_map/ppermute | solution.py:561
  271.9 40.5 %collective-permute-start.32 = (bf16[2,2,96,768]{3,2,1,0:T(8,128)(2,1)}, bf16[2,2,96,768]{3,2,1,0:T(8,128)(2,1)}, u32[]{:S(2)}, u32[]{:S(2)}) collective-permute-start(bf16[2,2,96,768]{3,2,1,0:T(8,128)(2,1)} %collective-permute-done.28.refs_6_), channel_id=1, source_target_pairs={{0,4},{4,0},{8,12},{12,8},{16,20},{20,16},{24,28},{28,24},{1,5},{5... | collective-permute-start | bytes 1769480 | tf_op jit(solution)/shard_map/ppermute | solution.py:561
  373.1 41.4 %collective-permute-start.45 = (bf16[608,768]{1,0:T(8,128)(2,1)}, bf16[608,768]{1,0:T(8,128)(2,1)}, u32[]{:S(2)}, u32[]{:S(2)}) collective-permute-start(bf16[608,768]{1,0:T(8,128)(2,1)} %get-tuple-element.136), channel_id=1, source_target_pairs={{0,2},{1,3},{2,0},{3,1},{4,6},{5,7},{6,4},{7,5},{8,10},{9,11},{10,... | collective-permute-start | bytes 2801672 | tf_op jit(solution)/shard_map/ppermute | solution.py:561
  404.9 85.9 %collective-permute-start.50 = (bf16[2,2,384,768]{3,2,1,0:T(8,128)(2,1)}, bf16[2,2,384,768]{3,2,1,0:T(8,128)(2,1)}, u32[]{:S(2)}, u32[]{:S(2)}) collective-permute-start(bf16[2,2,384,768]{3,2,1,0:T(8,128)(2,1)} %get-tuple-element.68), channel_id=1, source_target_pairs={{0,4},{4,0},{8,12},{12,8},{16,20},{20,16},{24,28},{28,24},{1,5},{5... | collective-permute-start | bytes 7077896 | tf_op jit(solution)/shard_map/ppermute | solution.py:561
  464.7 58.0 %collective-permute-start.48 = (bf16[2,8,112,768]{3,2,1,0:T(8,128)(2,1)}, bf16[2,8,112,768]{3,2,1,0:T(8,128)(2,1)}, u32[]{:S(2)}, u32[]{:S(2)}) collective-permute-start(bf16[2,8,112,768]{3,2,1,0:T(8,128)(2,1)} %get-tuple-element.66), channel_id=1, source_target_pairs={{0,1},{1,0},{2,3},{3,2},{4,5},{5,4},{6,7},{7,6},{8,9},{9,8},{10,11... | collective-permute-start | bytes 8257544 | tf_op jit(solution)/shard_map/ppermute | solution.py:561
  464.7 54.0 %collective-permute-start.52 = (bf16[2,2,384,768]{3,2,1,0:T(8,128)(2,1)}, bf16[2,2,384,768]{3,2,1,0:T(8,128)(2,1)}, u32[]{:S(2)}, u32[]{:S(2)}) collective-permute-start(bf16[2,2,384,768]{3,2,1,0:T(8,128)(2,1)} %get-tuple-element.70), channel_id=1, source_target_pairs={{0,4},{4,0},{8,12},{12,8},{16,20},{20,16},{24,28},{28,24},{1,5},{5... | collective-permute-start | bytes 7077896 | tf_op jit(solution)/shard_map/ppermute | solution.py:561
  490.6 116.0 %collective-permute-start.40 = (bf16[4,608,768]{2,1,0:T(8,128)(2,1)}, bf16[4,608,768]{2,1,0:T(8,128)(2,1)}, u32[]{:S(2)}, u32[]{:S(2)}) collective-permute-start(bf16[4,608,768]{2,1,0:T(8,128)(2,1)} %get-tuple-element.55), channel_id=1, source_target_pairs={{0,1},{1,0},{2,3},{3,2},{4,5},{5,4},{6,7},{7,6},{8,9},{9,8},{10,11... | collective-permute-start | bytes 11206664 | tf_op jit(solution)/shard_map/ppermute | solution.py:561
  492.3 80.3 %collective-permute-start.51 = (bf16[2,2,192,768]{3,2,1,0:T(8,128)(2,1)S(1)}, bf16[2,2,192,768]{3,2,1,0:T(8,128)(2,1)S(1)}, u32[]{:S(2)}, u32[]{:S(2)}) collective-permute-start(bf16[2,2,192,768]{3,2,1,0:T(8,128)(2,1)S(1)} %slice_add_fusion.4), channel_id=1, source_target_pairs={{0,16},{4,20},{8,24},{12,28},{16,0},{20,4},{24,8},{28,12},{1,17},{... | collective-permute-start | bytes 3538952 | tf_op jit(solution)/shard_map/ppermute | solution.py:561
  520.1 77.3 %collective-permute-start.53 = (bf16[2,2,192,768]{3,2,1,0:T(8,128)(2,1)S(1)}, bf16[2,2,192,768]{3,2,1,0:T(8,128)(2,1)S(1)}, u32[]{:S(2)}, u32[]{:S(2)}) collective-permute-start(bf16[2,2,192,768]{3,2,1,0:T(8,128)(2,1)S(1)} %slice_add_fusion.2), channel_id=1, source_target_pairs={{0,16},{4,20},{8,24},{12,28},{16,0},{20,4},{24,8},{28,12},{1,17},{... | collective-permute-start | bytes 3538952 | tf_op jit(solution)/shard_map/ppermute | solution.py:561
  524.2 75.0 %collective-permute-start.49 = (bf16[8,112,768]{2,1,0:T(8,128)(2,1)S(1)}, bf16[8,112,768]{2,1,0:T(8,128)(2,1)S(1)}, u32[]{:S(2)}, u32[]{:S(2)}) collective-permute-start(bf16[8,112,768]{2,1,0:T(8,128)(2,1)S(1)} %fusion.5), channel_id=1, source_target_pairs={{0,2},{1,3},{2,0},{3,1},{4,6},{5,7},{6,4},{7,5},{8,10},{9,11},{10,... | collective-permute-start | bytes 4128776 | tf_op jit(solution)/shard_map/ppermute | solution.py:561
  575.4 40.5 %collective-permute-start.54 = (bf16[2,2,96,768]{3,2,1,0:T(8,128)(2,1)}, bf16[2,2,96,768]{3,2,1,0:T(8,128)(2,1)}, u32[]{:S(2)}, u32[]{:S(2)}) collective-permute-start(bf16[2,2,96,768]{3,2,1,0:T(8,128)(2,1)} %get-tuple-element.150), channel_id=1, source_target_pairs={{0,8},{4,12},{8,0},{12,4},{16,24},{20,28},{24,16},{28,20},{1,9},{5... | collective-permute-start | bytes 1769480 | tf_op jit(solution)/shard_map/ppermute | solution.py:561
  601.9 69.3 %all-to-all-start = ((bf16[8,112,768]{2,1,0:T(8,128)(2,1)}), bf16[8,112,768]{2,1,0:T(8,128)(2,1)S(1)}, u32[]{:S(2)}, u32[]{:S(2)}) async-start(bf16[8,112,768]{2,1,0:T(8,128)(2,1)} %fusion.7), calls=%async_computation | async-start | bytes 2752512 | tf_op jit(solution)/shard_map/all_to_all | solution.py:723
  614.4 39.0 %collective-permute-start.41 = (bf16[608,768]{1,0:T(8,128)(2,1)}, bf16[608,768]{1,0:T(8,128)(2,1)S(1)}, u32[]{:S(2)}, u32[]{:S(2)}) collective-permute-start(bf16[608,768]{1,0:T(8,128)(2,1)} %get-tuple-element.139), channel_id=1, source_target_pairs={{0,2},{1,3},{2,0},{3,1},{4,6},{5,7},{6,4},{7,5},{8,10},{9,11},{10,... | collective-permute-start | bytes 2801672 | tf_op jit(solution)/shard_map/ppermute | solution.py:561
  (55 other events, 1013.6 us)
